TPU v7x, 128 devices: a whole 4x4x4 slice. The times are simulated.
128 devices in a mesh: tm: 8 (over z_hi, x), chan: 16 (over y, z_lo, core).
Axes of the slice: x: 4, y: 4, z: 4 (z_hi: 2, z_lo: 2; z = z_hi * 2 + z_lo), core: 2. Of those that a mesh axis runs over, the one named last changes fastest.
Arguments:
- strain: float32 [1024, 65536], P('chan', 'tm'), may hold values from -6 to 6
- fir_taps: float32 [64], replicated, may hold values from -0.75 to 0.75
- source_index: int32 [64], replicated, may hold values from 0 to 1023, as said below
Outputs:
- correlation: float32 [1024, 64, 512], P(('chan', 'tm'))
Inputs may be any that keep to these rules, and one draw needn't show every extreme that they name: `source_index`: point numbers; both 0 and 1023 occur, others may repeat.
All inputs are finite; a program needn't handle non-finite values.
Results may differ from a plain program's by a relative error of at most 0.0003.
Values sent between devices are 32-bit elements; how exact they have to be, the bound alone decides.
A program may use at most 128 MiB of HBM per device.

v0:
```python
import jax
import jax.numpy as jnp
from jax import lax
from jax.sharding import PartitionSpec as P

P_SIZE = 128
Q = 128
TAPS = 64
LAG_ROWS = 4
NT = 16384


white_floor = 0.1


def from_behind(value, axis, steps):
    count = lax.axis_size(axis)
    initial, last = (max(0, -steps), min(count, count - steps))
    return lax.ppermute(value, axis, [(source, source + steps) for source in range(initial, last)])


def tables(size_a, size_b, total):
    first = jnp.arange(size_a, dtype=jnp.int32)
    second = jnp.arange(size_b, dtype=jnp.int32)
    phase = (first[:, None] * second[None, :] % total).astype(jnp.float32)
    angle = 2.0 * jnp.pi / total * phase
    return (jnp.cos(angle), jnp.sin(angle))


def lag_tables():
    rows = (jnp.arange(LAG_ROWS, dtype=jnp.int32) + Q - LAG_ROWS // 2) % Q
    cols = jnp.arange(Q, dtype=jnp.int32)
    phase = (rows[:, None] * cols[None, :] % Q).astype(jnp.float32)
    angle = 2.0 * jnp.pi / Q * phase
    return (jnp.cos(angle), jnp.sin(angle))


def forward(series):
    high = lax.Precision.HIGHEST
    cos_q, sin_q = tables(Q, Q, Q)
    part_re = jnp.einsum("kq,bqp->bkp", cos_q, series, precision=high)
    part_im = -jnp.einsum("kq,bqp->bkp", sin_q, series, precision=high)
    cos_t, sin_t = tables(Q, P_SIZE, NT)
    turn_re = part_re * cos_t + part_im * sin_t
    turn_im = part_im * cos_t - part_re * sin_t
    cos_p, sin_p = tables(P_SIZE, P_SIZE, P_SIZE)
    spec_re = jnp.einsum("bkm,mn->bkn", turn_re, cos_p, precision=high) + jnp.einsum(
        "bkm,mn->bkn", turn_im, sin_p, precision=high
    )
    spec_im = jnp.einsum("bkm,mn->bkn", turn_im, cos_p, precision=high) - jnp.einsum(
        "bkm,mn->bkn", turn_re, sin_p, precision=high
    )
    return (spec_re, spec_im)


def whiten(spec_re, spec_im):
    energy = spec_re * spec_re + spec_im * spec_im
    power = jnp.mean(energy, axis=(1, 2), keepdims=True)
    denom = jnp.sqrt(energy + white_floor * power)
    return (spec_re / denom, spec_im / denom)


def correlate(chan_re, chan_im, src_re, src_im):
    high = lax.Precision.HIGHEST
    prod_re = src_re * chan_re + src_im * chan_im
    prod_im = src_re * chan_im - src_im * chan_re
    cos_p, sin_p = tables(P_SIZE, P_SIZE, P_SIZE)
    back_re = jnp.einsum("skn,nm->skm", prod_re, cos_p, precision=high) - jnp.einsum(
        "skn,nm->skm", prod_im, sin_p, precision=high
    )
    back_im = jnp.einsum("skn,nm->skm", prod_im, cos_p, precision=high) + jnp.einsum(
        "skn,nm->skm", prod_re, sin_p, precision=high
    )
    cos_t, sin_t = tables(Q, P_SIZE, NT)
    turn_re = back_re * cos_t - back_im * sin_t
    turn_im = back_im * cos_t + back_re * sin_t
    cos_l, sin_l = lag_tables()
    lagged = jnp.einsum("rk,skm->srm", cos_l, turn_re, precision=high) - jnp.einsum(
        "rk,skm->srm", sin_l, turn_im, precision=high
    )
    return lagged.reshape(lagged.shape[0], LAG_ROWS * P_SIZE) * (1.0 / jnp.sqrt(jnp.float32(NT)))


def filter_blocks(padded, fir_taps, count):
    blocks = TAPS // 4
    matrix = fir_taps.reshape(blocks, 4)[:, ::-1]
    total = jnp.zeros((padded.shape[0], count), jnp.float32)
    for offset in range(blocks):
        start = blocks - 1 - offset
        total = total + jnp.sum(padded[:, start : start + count, :] * matrix[offset], axis=-1)
    return total


def on_device(strain, fir_taps, source_index):
    group_rows, width = strain.shape
    count = width // 4
    tail = strain[:, width - TAPS :]
    earlier = from_behind(tail, "tm", 1)
    joined = jnp.concatenate([earlier[:, 4:], strain], axis=1)
    padded = joined.reshape(group_rows, count + TAPS // 4 - 1, 4)
    decimated = filter_blocks(padded, fir_taps, count)
    turned = lax.all_to_all(decimated, "tm", split_axis=0, concat_axis=1, tiled=True)
    local = turned.shape[0]
    spec_re, spec_im = forward(turned.reshape(local, Q, P_SIZE))
    white_re, white_im = whiten(spec_re, spec_im)
    high = lax.Precision.HIGHEST
    first_local = lax.axis_index("chan") * group_rows + lax.axis_index("tm") * local
    owned = jnp.arange(local, dtype=jnp.int32) + first_local
    picker = (source_index[:, None] == owned[None, :]).astype(jnp.float32)
    part_re = jnp.einsum("sc,ckp->skp", picker, white_re, precision=high)
    part_im = jnp.einsum("sc,ckp->skp", picker, white_im, precision=high)
    src_re, src_im = lax.psum((part_re, part_im), ("tm", "chan"))

    def one_channel(pair):
        return correlate(pair[0], pair[1], src_re, src_im)

    return lax.map(one_channel, (white_re, white_im))


def solution(mesh):
    in_specs = (P("chan", "tm"), P(), P())
    out_specs = P(("chan", "tm"), None, None)
    return jax.shard_map(
        on_device, mesh=mesh, in_specs=in_specs, out_specs=out_specs, check_vma=False
    )
```

profile of v0, /device:TPU:1, one launch (start us, length us, event | category | flops | bytes accessed | tf_op | source)
XLA Modules:
  0.0 529.1 jit_solution(13311487390221544274)
XLA Ops:
  7.4 3.9 collective-permute-start
  11.3 1.3 fusion.165
  14.3 2.2 pad_maximum_fusion
  16.5 3.3 copy.41
  19.7 5.5 %reshape.202 = f32[64,2063,4]{0,2,1:T(4,128)} reshape(f32[64,8252]{0,1:T(8,128)} %copy.41) | data formatting | bytes 4225024 | tf_op jit(solution)/shard_map/reshape | solution.py:100
  25.2 37.7 %fusion.95 = (f32[64,2048]{0,1:T(8,128)S(1)}, f32[64,2048]{0,1:T(8,128)S(1)}, f32[64,2048]{0,1:T(8,128)}, f32[64,2048]{0,1:T(8,128)}, f32[64,2048]{0,1:T(8,128)}, /*index=5*/f32[64,2048]{0,1:T(8,128)}, f32[64,2048]{0,1:T(8,128)}) fusion(f32[64,2063,4]{0,2,1:T(4,128)} %reshape.202, f32[4]{0:T(128)S(1)} %reverse.64, f32[4]{0:T(128)S(1)} %reverse.71, ...), kind=kLoop, calls=%fused_computation.118 | loop fusion | flops 6422528 | bytes 18350192 | tf_op jit(solution)/shard_map/reduce_sum | solution.py:90
  62.9 42.2 %fusion.94 = (f32[64,2048]{0,1:T(8,128)}, f32[64,2048]{0,1:T(8,128)}, f32[64,2048]{0,1:T(8,128)}, f32[64,2048]{0,1:T(8,128)}, f32[64,2048]{0,1:T(8,128)}, /*inde...) fusion(f32[64,2063,4]{0,2,1:T(4,128)S(1)} %copy-done.2, f32[4]{0:T(128)S(1)} %reverse.65, ...), kind=kLoop, calls=%fused_computation.116 | loop fusion | flops 8257536 | bytes 23593104 | tf_op jit(solution)/shard_map/reduce_sum | solution.py:90
  105.2 6.0 %add_add_fusion = f32[64,2048]{0,1:T(8,128)S(1)} fusion(f32[64,2048]{0,1:T(8,128)} %get-tuple-element.180, f32[64,2048]{0,1:T(8,128)} %get-tuple-element.181, f32[64,2048]{0,1:T(8,128)} %get-tuple-element.182, f32[64,2048]{0,1:T(8,128)} %get-tuple-element.183, f32[64,2048]{0,1:T(8,128)} %get-tuple-element.184, f32[64,2048]{0,1:T(8,128)} %get-tuple-element.185, ...), kind=kLoop, calls=%fused_computation.125 | loop fusion | flops 1966080 | bytes 8912896 | tf_op jit(solution)/shard_map/add | solution.py:90
  112.2 7.1 %all-to-all-start = ((f32[8,8,2048]{2,1,0:T(8,128)}), f32[8,8,2048]{2,1,0:T(8,128)S(1)}, u32[]{:S(2)}, u32[]{:S(2)}) async-start(f32[8,8,2048]{2,1,0:T(8,128)} %bitcast.7), calls=%async_computation | async-start | bytes 1048576 | tf_op jit(solution)/shard_map/all_to_all | solution.py:102
  120.2 9.0 %all-to-all-done = f32[8,8,2048]{2,1,0:T(8,128)S(1)} async-done(((f32[8,8,2048]{2,1,0:T(8,128)}), f32[8,8,2048]{2,1,0:T(8,128)S(1)}, u32[]{:S(2)}, u32[]{:S(2)}) %all-to-all-start) | async-done | bytes 524320 | tf_op jit(solution)/shard_map/all_to_all | solution.py:102
  137.0 3.9 fusion.97
  140.9 4.0 fusion.99
  144.9 161.5 %all-reduce.3.cloned.1.call-done = (f32[64,128,128]{2,0,1:T(8,128)}, f32[64,128,128]{2,0,1:T(8,128)}) async-done(((f32[64,128,128]{2,0,1:T(8,128)}, f32[64,128,128]{2,0,1:T(8,128)}), (f32[64,128,128]{2,0,1:T(8,128)}, f32[64,128,128]{2,0,1:T(8,128)})) %all-reduce.3.cloned.1.call-update) | async-done | bytes 8388624 | tf_op jit(solution)/shard_map/psum | solution.py:112
  306.4 6.7 %copy.54 = f32[64,128,128]{2,1,0:T(8,128)} copy(f32[64,128,128]{2,0,1:T(8,128)} %get-tuple-element.207) | data formatting | bytes 8388608 | tf_op jit(solution)/shard_map/while | solution.py:117
  313.1 4.4 copy.55
  317.5 204.3 %while.15 = (s32[]{:T(128)}, f32[8,64,512]{2,1,0:T(8,128)}, f32[8,128,128]{2,1,0:T(8,128)S(1)}, f32[64,128,128]{2,1,0:T(8,128)}, f32[8,128,128]{2,1,0:T(8,128)S(1)}, /*index=5*/f32[64,128,128]{2,1,0:T(8,128)}, s32[]{:T(128)}) while((s32[]{:T(128)}, f32[8,64,512]{2,1,0:T(8,128)}, f32[8,128,128]{2,1,0:T(8,128)S(1)}, ...), condition=%wide.region_20.21_spmd, body=%wide.region_19.20_spmd.sunk | while | flops 6565312512 | bytes 111149752 | solution.py:117
  317.8 6.8 %fusion.190 = f32[64,128,128]{2,1,0:T(8,128)S(1)} fusion(f32[64,128,128]{2,1,0:T(8,128)} %get-tuple-element.297, f32[64,128,128]{2,1,0:T(8,128)} %get-tuple-element.295, f32[128,128]{1,0:T(8,128)S(1)} %get-tuple-element.274, f32[128,128]{1,0:T(8,128)S(1)} %get-tuple-element.275), kind=kOutput, calls=%fused_computation.17.clone.1 | convolution fusion | flops 1613987840 | bytes 12713984 | tf_op jit(solution)/shard_map/while/body/eval_jaxpr/skn,nm->skm/dot_general | solution.py:71
  324.6 4.1 convolution_add_fusion.3
  328.7 4.0 fusion.189
  332.7 4.1 convolution_subtract_fusion.3
  337.1 2.7 fusion.192
  339.8 2.7 fusion.193
  343.3 6.8 %fusion.190 = f32[64,128,128]{2,1,0:T(8,128)S(1)} fusion(f32[64,128,128]{2,1,0:T(8,128)} %get-tuple-element.297, f32[64,128,128]{2,1,0:T(8,128)} %get-tuple-element.295, f32[128,128]{1,0:T(8,128)S(1)} %get-tuple-element.274, f32[128,128]{1,0:T(8,128)S(1)} %get-tuple-element.275), kind=kOutput, calls=%fused_computation.17.clone.1 | convolution fusion | flops 1613987840 | bytes 12713984 | tf_op jit(solution)/shard_map/while/body/eval_jaxpr/skn,nm->skm/dot_general | solution.py:71
  350.1 4.1 convolution_add_fusion.3
  354.2 4.0 fusion.189
  358.2 4.1 convolution_subtract_fusion.3
  362.6 2.7 fusion.192
  365.3 2.7 fusion.193
  368.8 6.8 %fusion.190 = f32[64,128,128]{2,1,0:T(8,128)S(1)} fusion(f32[64,128,128]{2,1,0:T(8,128)} %get-tuple-element.297, f32[64,128,128]{2,1,0:T(8,128)} %get-tuple-element.295, f32[128,128]{1,0:T(8,128)S(1)} %get-tuple-element.274, f32[128,128]{1,0:T(8,128)S(1)} %get-tuple-element.275), kind=kOutput, calls=%fused_computation.17.clone.1 | convolution fusion | flops 1613987840 | bytes 12713984 | tf_op jit(solution)/shard_map/while/body/eval_jaxpr/skn,nm->skm/dot_general | solution.py:71
  375.6 4.1 convolution_add_fusion.3
  379.7 4.0 fusion.189
  383.7 4.1 convolution_subtract_fusion.3
  388.1 2.7 fusion.192
  390.8 2.7 fusion.193
  394.3 6.8 %fusion.190 = f32[64,128,128]{2,1,0:T(8,128)S(1)} fusion(f32[64,128,128]{2,1,0:T(8,128)} %get-tuple-element.297, f32[64,128,128]{2,1,0:T(8,128)} %get-tuple-element.295, f32[128,128]{1,0:T(8,128)S(1)} %get-tuple-element.274, f32[128,128]{1,0:T(8,128)S(1)} %get-tuple-element.275), kind=kOutput, calls=%fused_computation.17.clone.1 | convolution fusion | flops 1613987840 | bytes 12713984 | tf_op jit(solution)/shard_map/while/body/eval_jaxpr/skn,nm->skm/dot_general | solution.py:71
  401.1 4.1 convolution_add_fusion.3
  405.2 4.0 fusion.189
  409.2 4.1 convolution_subtract_fusion.3
  413.6 2.7 fusion.192
  416.3 2.7 fusion.193
  419.8 6.8 %fusion.190 = f32[64,128,128]{2,1,0:T(8,128)S(1)} fusion(f32[64,128,128]{2,1,0:T(8,128)} %get-tuple-element.297, f32[64,128,128]{2,1,0:T(8,128)} %get-tuple-element.295, f32[128,128]{1,0:T(8,128)S(1)} %get-tuple-element.274, f32[128,128]{1,0:T(8,128)S(1)} %get-tuple-element.275), kind=kOutput, calls=%fused_computation.17.clone.1 | convolution fusion | flops 1613987840 | bytes 12713984 | tf_op jit(solution)/shard_map/while/body/eval_jaxpr/skn,nm->skm/dot_general | solution.py:71
  426.6 4.1 convolution_add_fusion.3
  430.7 4.0 fusion.189
  434.7 4.1 convolution_subtract_fusion.3
  439.1 2.7 fusion.192
  441.9 2.7 fusion.193
  445.4 6.8 %fusion.190 = f32[64,128,128]{2,1,0:T(8,128)S(1)} fusion(f32[64,128,128]{2,1,0:T(8,128)} %get-tuple-element.297, f32[64,128,128]{2,1,0:T(8,128)} %get-tuple-element.295, f32[128,128]{1,0:T(8,128)S(1)} %get-tuple-element.274, f32[128,128]{1,0:T(8,128)S(1)} %get-tuple-element.275), kind=kOutput, calls=%fused_computation.17.clone.1 | convolution fusion | flops 1613987840 | bytes 12713984 | tf_op jit(solution)/shard_map/while/body/eval_jaxpr/skn,nm->skm/dot_general | solution.py:71
  452.1 4.1 convolution_add_fusion.3
  456.2 4.0 fusion.189
  460.2 4.1 convolution_subtract_fusion.3
  464.6 2.7 fusion.192
  467.4 2.7 fusion.193
  470.9 6.8 %fusion.190 = f32[64,128,128]{2,1,0:T(8,128)S(1)} fusion(f32[64,128,128]{2,1,0:T(8,128)} %get-tuple-element.297, f32[64,128,128]{2,1,0:T(8,128)} %get-tuple-element.295, f32[128,128]{1,0:T(8,128)S(1)} %get-tuple-element.274, f32[128,128]{1,0:T(8,128)S(1)} %get-tuple-element.275), kind=kOutput, calls=%fused_computation.17.clone.1 | convolution fusion | flops 1613987840 | bytes 12713984 | tf_op jit(solution)/shard_map/while/body/eval_jaxpr/skn,nm->skm/dot_general | solution.py:71
  477.7 4.1 convolution_add_fusion.3
  481.8 4.0 fusion.189
  485.8 4.1 convolution_subtract_fusion.3
  490.1 2.7 fusion.192
  492.9 2.7 fusion.193
  496.4 6.8 %fusion.190 = f32[64,128,128]{2,1,0:T(8,128)S(1)} fusion(f32[64,128,128]{2,1,0:T(8,128)} %get-tuple-element.297, f32[64,128,128]{2,1,0:T(8,128)} %get-tuple-element.295, f32[128,128]{1,0:T(8,128)S(1)} %get-tuple-element.274, f32[128,128]{1,0:T(8,128)S(1)} %get-tuple-element.275), kind=kOutput, calls=%fused_computation.17.clone.1 | convolution fusion | flops 1613987840 | bytes 12713984 | tf_op jit(solution)/shard_map/while/body/eval_jaxpr/skn,nm->skm/dot_general | solution.py:71
  503.2 4.1 convolution_add_fusion.3
  507.3 4.0 fusion.189
  511.3 4.1 convolution_subtract_fusion.3
  515.7 2.7 fusion.192
  518.4 2.7 fusion.193
  (116 shorter events, 20.4 us)
Async XLA Ops:
  7.4 6.8 %collective-permute-start = (f32[64,64]{1,0:T(8,128)S(1)}, f32[64,64]{1,0:T(8,128)S(1)}, u32[]{:S(2)}, u32[]{:S(2)}) collective-permute-start(f32[64,64]{1,0:T(8,128)S(1)} %slice.134), channel_id=1, source_target_pairs={{0,16},{16,32},{32,48},{48,64},{64,80},{80,96},{96,112},{1,17},{17... | collective-permute-start | bytes 49160 | tf_op jit(solution)/shard_map/ppermute | solution.py:19
  25.2 37.7 %copy-start.2 = (f32[64,2063,4]{0,2,1:T(4,128)S(1)}, f32[64,2063,4]{0,2,1:T(4,128)}, u32[]{:S(2)}) copy-start(f32[64,2063,4]{0,2,1:T(4,128)} %reshape.202) | copy-start | bytes 6337540
  112.2 16.9 %all-to-all-start = ((f32[8,8,2048]{2,1,0:T(8,128)}), f32[8,8,2048]{2,1,0:T(8,128)S(1)}, u32[]{:S(2)}, u32[]{:S(2)}) async-start(f32[8,8,2048]{2,1,0:T(8,128)} %bitcast.7), calls=%async_computation | async-start | bytes 1048576 | tf_op jit(solution)/shard_map/all_to_all | solution.py:102
  119.4 187.1 %all-reduce.3.cloned.1.call-start = ((), (), s32[]{:S(2)}) async-start(), calls=%async_computation.1 | async-start | bytes 16777216 | tf_op jit(solution)/shard_map/psum | solution.py:112
  133.0 4.0 copy-start.4
  306.4 6.7 %copy-start.3 = (f32[64,128,128]{2,0,1:T(8,128)S(1)}, f32[64,128,128]{2,0,1:T(8,128)}, u32[]{:S(2)}) copy-start(f32[64,128,128]{2,0,1:T(8,128)} %get-tuple-element.208) | copy-start | bytes 12582916
  317.8 6.8 %copy-start = (f32[64,128,128]{2,1,0:T(8,128)S(1)}, f32[64,128,128]{2,1,0:T(8,128)}, u32[]{:S(2)}) copy-start(f32[64,128,128]{2,1,0:T(8,128)} %get-tuple-element.295) | copy-start | bytes 12582916 | tf_op jit(solution)/shard_map/while
  317.8 6.8 %copy-start.1 = (f32[64,128,128]{2,1,0:T(8,128)S(1)}, f32[64,128,128]{2,1,0:T(8,128)}, u32[]{:S(2)}) copy-start(f32[64,128,128]{2,1,0:T(8,128)} %get-tuple-element.297) | copy-start | bytes 12582916 | tf_op jit(solution)/shard_map/while
  343.3 6.8 %copy-start = (f32[64,128,128]{2,1,0:T(8,128)S(1)}, f32[64,128,128]{2,1,0:T(8,128)}, u32[]{:S(2)}) copy-start(f32[64,128,128]{2,1,0:T(8,128)} %get-tuple-element.295) | copy-start | bytes 12582916 | tf_op jit(solution)/shard_map/while
  343.3 6.8 %copy-start.1 = (f32[64,128,128]{2,1,0:T(8,128)S(1)}, f32[64,128,128]{2,1,0:T(8,128)}, u32[]{:S(2)}) copy-start(f32[64,128,128]{2,1,0:T(8,128)} %get-tuple-element.297) | copy-start | bytes 12582916 | tf_op jit(solution)/shard_map/while
  368.8 6.8 %copy-start = (f32[64,128,128]{2,1,0:T(8,128)S(1)}, f32[64,128,128]{2,1,0:T(8,128)}, u32[]{:S(2)}) copy-start(f32[64,128,128]{2,1,0:T(8,128)} %get-tuple-element.295) | copy-start | bytes 12582916 | tf_op jit(solution)/shard_map/while
  368.8 6.8 %copy-start.1 = (f32[64,128,128]{2,1,0:T(8,128)S(1)}, f32[64,128,128]{2,1,0:T(8,128)}, u32[]{:S(2)}) copy-start(f32[64,128,128]{2,1,0:T(8,128)} %get-tuple-element.297) | copy-start | bytes 12582916 | tf_op jit(solution)/shard_map/while
  394.3 6.8 %copy-start = (f32[64,128,128]{2,1,0:T(8,128)S(1)}, f32[64,128,128]{2,1,0:T(8,128)}, u32[]{:S(2)}) copy-start(f32[64,128,128]{2,1,0:T(8,128)} %get-tuple-element.295) | copy-start | bytes 12582916 | tf_op jit(solution)/shard_map/while
  394.3 6.8 %copy-start.1 = (f32[64,128,128]{2,1,0:T(8,128)S(1)}, f32[64,128,128]{2,1,0:T(8,128)}, u32[]{:S(2)}) copy-start(f32[64,128,128]{2,1,0:T(8,128)} %get-tuple-element.297) | copy-start | bytes 12582916 | tf_op jit(solution)/shard_map/while
  419.8 6.8 %copy-start = (f32[64,128,128]{2,1,0:T(8,128)S(1)}, f32[64,128,128]{2,1,0:T(8,128)}, u32[]{:S(2)}) copy-start(f32[64,128,128]{2,1,0:T(8,128)} %get-tuple-element.295) | copy-start | bytes 12582916 | tf_op jit(solution)/shard_map/while
  419.8 6.8 %copy-start.1 = (f32[64,128,128]{2,1,0:T(8,128)S(1)}, f32[64,128,128]{2,1,0:T(8,128)}, u32[]{:S(2)}) copy-start(f32[64,128,128]{2,1,0:T(8,128)} %get-tuple-element.297) | copy-start | bytes 12582916 | tf_op jit(solution)/shard_map/while
  445.3 6.8 %copy-start = (f32[64,128,128]{2,1,0:T(8,128)S(1)}, f32[64,128,128]{2,1,0:T(8,128)}, u32[]{:S(2)}) copy-start(f32[64,128,128]{2,1,0:T(8,128)} %get-tuple-element.295) | copy-start | bytes 12582916 | tf_op jit(solution)/shard_map/while
  445.3 6.8 %copy-start.1 = (f32[64,128,128]{2,1,0:T(8,128)S(1)}, f32[64,128,128]{2,1,0:T(8,128)}, u32[]{:S(2)}) copy-start(f32[64,128,128]{2,1,0:T(8,128)} %get-tuple-element.297) | copy-start | bytes 12582916 | tf_op jit(solution)/shard_map/while
  470.8 6.8 %copy-start = (f32[64,128,128]{2,1,0:T(8,128)S(1)}, f32[64,128,128]{2,1,0:T(8,128)}, u32[]{:S(2)}) copy-start(f32[64,128,128]{2,1,0:T(8,128)} %get-tuple-element.295) | copy-start | bytes 12582916 | tf_op jit(solution)/shard_map/while
  470.9 6.8 %copy-start.1 = (f32[64,128,128]{2,1,0:T(8,128)S(1)}, f32[64,128,128]{2,1,0:T(8,128)}, u32[]{:S(2)}) copy-start(f32[64,128,128]{2,1,0:T(8,128)} %get-tuple-element.297) | copy-start | bytes 12582916 | tf_op jit(solution)/shard_map/while
  496.4 6.8 %copy-start = (f32[64,128,128]{2,1,0:T(8,128)S(1)}, f32[64,128,128]{2,1,0:T(8,128)}, u32[]{:S(2)}) copy-start(f32[64,128,128]{2,1,0:T(8,128)} %get-tuple-element.295) | copy-start | bytes 12582916 | tf_op jit(solution)/shard_map/while
  496.4 6.8 %copy-start.1 = (f32[64,128,128]{2,1,0:T(8,128)S(1)}, f32[64,128,128]{2,1,0:T(8,128)}, u32[]{:S(2)}) copy-start(f32[64,128,128]{2,1,0:T(8,128)} %get-tuple-element.297) | copy-start | bytes 12582916 | tf_op jit(solution)/shard_map/while
Sparse Core Ops, SparseCore 0:
  145.0 161.3 all-reduce.2
where the time goes:
time: 539 us; the launch traced here: 529 us
  matrix products  210 us (39%)
  waiting for transfers between devices  170 us (32%)
  other arithmetic  91.2 us (17%)
  local copies, waits for them, and re-layouts  31.3 us (6%)
  between operations  13.9 us (3%)
  starting transfers between devices  11.1 us (2%)
    psum x1, waiting for transfers between devices, on_device(): src_re, src_im = lax.psum((part_re, part_im), ('tm', 'chan'))  162 us
    reduce_sum x2, other arithmetic, filter_blocks(): jnp.sum(padded[:, start:start + count, :] * matrix[offset], axis=-1)  79.9 us
    dot_general x8, matrix products, correlate(): jnp.einsum('skn,nm->skm', prod_im, cos_p, precision=high)  54.1 us
    dot_general x8, matrix products, correlate(): jnp.einsum('skn,nm->skm', prod_re, sin_p, precision=high)  32.8 us
    dot_general x8, matrix products, correlate(): jnp.einsum('skn,nm->skm', prod_im, sin_p, precision=high)  32.8 us
    dot_general x8, matrix products, correlate(): jnp.einsum('skn,nm->skm', prod_re, cos_p, precision=high)  31.9 us
    dot_general x8, matrix products, correlate(): jnp.einsum('rk,skm->srm', cos_l, turn_re, precision=high)  21.8 us
    dot_general x8, matrix products, correlate(): jnp.einsum('rk,skm->srm', sin_l, turn_im, precision=high)  21.8 us
  transfers between devices with their start and end apart: 3, of which 2 were waited for; matrix products, arithmetic and copies ran while one was open for 1% of the time, Pallas kernels for 0%

commit v1 on v0

v1 whole, which is shorter than its diff:
```python
import functools

import jax
import jax.numpy as jnp
import ml_dtypes
import numpy as np
from jax import lax
from jax.experimental import pallas as pl
from jax.experimental.pallas import tpu as pltpu
from jax.sharding import PartitionSpec as P

MESH = pl.DeviceIdType.MESH
VMEM = pltpu.VMEM
N = 128
NT = N * N
HALF = N // 2
TAPS = 64
NSRC = 64
FLOOR = 0.1
LAG_ROWS = 4
GROUP = 64
TM = 8
BLOCKS = 16
SPILL = BLOCKS
BAND = 5 * N
RS = BLOCKS // 2 + 1
KINDS = ((0, 24, "xyz"), (24, 24, "yzx"), (48, 16, "zxy"))
VMEM_LIMIT = 56 * 1024 * 1024


def split_np(table):
    high = table.astype(np.float32).astype(ml_dtypes.bfloat16)
    low = (table - high.astype(np.float64)).astype(np.float32).astype(ml_dtypes.bfloat16)
    return high, low


def stack_np(table):
    return np.stack(split_np(table))


def series_tables():
    k = np.arange(HALF)[:, None]
    q = np.arange(N)[None, :]
    ang = 2 * np.pi * ((k * q) % N) / N
    first = np.concatenate([np.cos(ang), -np.sin(ang)])
    first[HALF] = np.cos(np.pi * np.arange(N))
    ang = 2 * np.pi * ((np.arange(N)[:, None] * np.arange(N)[None, :]) % N) / N
    c, s = np.cos(ang), np.sin(ang)
    second = np.block([[c, -s], [s, c]])
    third = np.block([[c, s], [-s, c]])
    ang = 2 * np.pi * ((np.arange(N)[:, None] * np.arange(HALF)[None, :]) % N) / N
    last = np.concatenate([2 * np.cos(ang), -2 * np.sin(ang)], axis=1) / N
    last[:, 0] = 1.0 / N
    last[:, HALF] = np.cos(np.pi * np.arange(N)) / N
    ang = 2 * np.pi * (np.arange(HALF + 8)[:, None] * np.arange(N)[None, :]) / NT
    turn = np.stack([np.cos(ang), np.sin(ang)]).astype(np.float32)
    return first, second, third, last, turn


def window_tables():
    f = np.arange(N)[:, None]
    u = np.arange(2 * N)[None, :]
    ang = 2 * np.pi * ((f * u) % (2 * N)) / (2 * N)
    win = np.concatenate([np.cos(ang), -np.sin(ang)])
    win[N] = np.cos(np.pi * np.arange(2 * N))
    m = np.arange(N)[None, :]
    ang = 2 * np.pi * ((f * m) % (2 * N)) / (2 * N)
    scale = 1.0 / (2 * N * N)
    back = np.concatenate([2 * np.cos(ang), -2 * np.sin(ang)]) * scale
    back[0] = scale
    back[N] = np.cos(np.pi * np.arange(N)) * scale
    return win, back


def split(value):
    high = value.astype(jnp.bfloat16)
    low = (value - high.astype(jnp.float32)).astype(jnp.bfloat16)
    return high, low


def mm(a, b):
    return jnp.dot(a, b, preferred_element_type=jnp.float32)


def mm3(a, b):
    return mm(a[0], b[0]) + mm(a[0], b[1]) + mm(a[1], b[0])


def filter_kernel(strain_ref, taps_ref, index_ref, dec_ref, src_ref, band):
    rho = lax.broadcasted_iota(jnp.int32, (8, N), 0)
    lane = lax.broadcasted_iota(jnp.int32, (8, N), 1)
    shifted = 4 * lane - rho
    base = jnp.zeros((8, N), jnp.float32)
    for j in range(TAPS):
        base = base + jnp.where(shifted == j - 3, taps_ref[j], 0.0)
    base = jnp.where(shifted >= -3, base, 0.0)
    for t in range(BAND // 8):
        move = 2 * t - 32
        tap = 4 * lane + (131 - 8 * t) - rho
        rolled = base if move % N == 0 else pltpu.roll(base, move % N, 1)
        rows = jnp.where((tap >= 0) & (tap < TAPS), rolled, 0.0)
        band[8 * t : 8 * t + 8, :] = rows
    b_hi, b_lo = split(band[...])
    both = jnp.concatenate([b_hi, b_lo], axis=1)

    base_channel = lax.axis_index("chan") * GROUP
    owned = lax.broadcasted_iota(jnp.int32, (NSRC, 2 * GROUP), 1) % GROUP + base_channel
    picker = jnp.where(index_ref[...] == owned, 1.0, 0.0).astype(jnp.bfloat16)

    def finish(block, out):
        for j in range(TM):
            dec_ref[j, block] = out[8 * j : 8 * j + 8]
        picked = mm(picker, jnp.concatenate(split(out), axis=0))
        for j in range(NSRC // 8):
            src_ref[j, block] = picked[8 * j : 8 * j + 8]

    step = 4
    for b0 in range(0, BLOCKS, step):
        his, los = [], []
        for b in range(b0, b0 + step):
            if b == 0:
                x = jnp.concatenate([jnp.zeros((GROUP, N), jnp.float32), strain_ref[:, : 4 * N]], axis=1)
            else:
                x = strain_ref[:, 4 * N * b - N : 4 * N * (b + 1)]
            hi, lo = split(x)
            his.append(hi)
            los.append(lo)
        hi = jnp.concatenate(his, axis=0)
        lo = jnp.concatenate(los, axis=0)
        wide = mm(hi, both)
        out = wide[:, :N] + wide[:, N:] + mm(lo, b_hi)
        for b in range(b0, b0 + step):
            finish(b, out[GROUP * (b - b0) : GROUP * (b - b0 + 1)])
    hi, lo = split(strain_ref[:, 4 * N * BLOCKS - N :])
    wide = mm(hi, both[:N])
    finish(SPILL, wide[:, :N] + wide[:, N:] + mm(lo, b_hi[:N]))


def run_filter(strain, fir_taps, source_index):
    return pl.pallas_call(
        filter_kernel,
        out_shape=[jax.ShapeDtypeStruct((8, BLOCKS + 1, 8, N), jnp.float32)] * 2,
        in_specs=[
            pl.BlockSpec(memory_space=VMEM),
            pl.BlockSpec(memory_space=pltpu.SMEM),
            pl.BlockSpec(memory_space=VMEM),
        ],
        out_specs=[pl.BlockSpec(memory_space=VMEM)] * 2,
        scratch_shapes=[VMEM((BAND, N), jnp.float32)],
        compiler_params=pltpu.CompilerParams(vmem_limit_bytes=VMEM_LIMIT),
        name="decimate",
    )(strain, fir_taps, source_index.reshape(NSRC, 1))


def exchange_kernel(dec_ref, src_ref, chan_out, rows_out, rs_buf, acc, row_buf, d_send, d_recv, s_send, s_recv, r_send, r_recv, own_sem):
    tm = lax.axis_index("tm")
    ch = lax.axis_index("chan")
    pair = ch // 2
    core = ch % 2
    peers = [((tm + d) % TM, ch) for d in range(1, TM)]
    peers += [(tm, (ch + d) % 16) for d in range(1, 16)]
    peers += [((tm + d) % TM, 2 * pair + 1 - core) for d in range(1, TM)]
    barrier = pltpu.get_barrier_semaphore()
    for peer in peers:
        pl.semaphore_signal(barrier, inc=1, device_id=peer, device_id_type=MESH)
    pl.semaphore_wait(barrier, len(peers))

    copies = []
    picks = []
    for d in range(1, 16):
        other = (ch + d) % 16
        copy = pltpu.make_async_remote_copy(
            src_ref=src_ref.at[other // 2, pl.ds((other % 2) * (RS - 1), RS)],
            dst_ref=rs_buf.at[d],
            send_sem=s_send.at[d],
            recv_sem=s_recv.at[d],
            device_id=(tm, other),
            device_id_type=MESH,
        )
        copy.start()
        picks.append(copy)
    for d in range(1, TM):
        other = (tm + d) % TM
        copy = pltpu.make_async_remote_copy(
            src_ref=dec_ref.at[other],
            dst_ref=chan_out.at[tm],
            send_sem=d_send.at[d],
            recv_sem=d_recv.at[d],
            device_id=(other, ch),
            device_id_type=MESH,
        )
        copy.start()
        copies.append(copy)
    own = pltpu.make_async_copy(dec_ref.at[tm], chan_out.at[tm], own_sem.at[0])
    own.start()
    for copy in picks:
        copy.wait_recv()
    total = src_ref[pair, pl.ds(core * (RS - 1), RS)]
    for d in range(1, 16):
        total = total + rs_buf[d]
    acc[...] = total.reshape(RS * 8, N)
    for j in range(TM):
        row_buf[j, :RS] = acc[pl.ds(j, RS, stride=8), :]
        row_buf[j, RS:] = jnp.zeros((16 - RS, N), jnp.float32)
    rows = []
    for d in range(TM):
        for e in range(2):
            if d == 0 and e == 0:
                continue
            other = (tm + d) % TM
            copy = pltpu.make_async_remote_copy(
                src_ref=row_buf.at[other],
                dst_ref=rows_out.at[core, tm],
                send_sem=r_send.at[d, e],
                recv_sem=r_recv.at[d, e],
                device_id=(other, 2 * pair + (core + e) % 2),
                device_id_type=MESH,
            )
            copy.start()
            rows.append(copy)
    mine = pltpu.make_async_copy(row_buf.at[tm], rows_out.at[core, tm], own_sem.at[1])
    mine.start()
    for copy in picks:
        copy.wait_send()
    for copy in copies + rows:
        copy.wait()
    own.wait()
    mine.wait()


def run_exchange(dec, src):
    dma = pltpu.SemaphoreType.DMA
    return pl.pallas_call(
        exchange_kernel,
        out_shape=[
            jax.ShapeDtypeStruct((TM, BLOCKS + 1, 8, N), jnp.float32),
            jax.ShapeDtypeStruct((2, TM, 16, N), jnp.float32),
        ],
        in_specs=[pl.BlockSpec(memory_space=VMEM)] * 2,
        out_specs=[pl.BlockSpec(memory_space=VMEM)] * 2,
        scratch_shapes=[
            VMEM((16, RS, 8, N), jnp.float32),
            VMEM((RS * 8, N), jnp.float32),
            VMEM((TM, 16, N), jnp.float32),
            dma((TM,)),
            dma((TM,)),
            dma((16,)),
            dma((16,)),
            dma((TM, 2)),
            dma((TM, 2)),
            dma((2,)),
        ],
        compiler_params=pltpu.CompilerParams(collective_id=0, has_side_effects=True, vmem_limit_bytes=VMEM_LIMIT),
        name="exchange",
    )(dec, src)


def whiten_series(series, first, second, third, last, turn):
    count = len(series)
    powers = [jnp.sum(x * x) for x in series]
    x_hi, x_lo = split(jnp.concatenate(series, axis=1))
    a_hi, a_lo = first[0], first[1]
    part = mm(jnp.concatenate([a_hi, a_hi], axis=1), jnp.concatenate([x_hi, x_lo], axis=0)) + mm(a_lo, x_hi)
    cos, sin = turn[0, :HALF], turn[1, :HALF]
    cos_mid, sin_mid = turn[0, HALF : HALF + 1], turn[1, HALF : HALF + 1]
    top = lax.broadcasted_iota(jnp.int32, (HALF, N), 0) == 0
    cos_im = jnp.where(top, 0.0, cos)
    rows, mids = [], []
    for i in range(count):
        re = part[:HALF, N * i : N * (i + 1)]
        im = part[HALF:, N * i : N * (i + 1)]
        rows.append(jnp.concatenate([re * cos + im * sin, im * cos_im - re * sin], axis=1))
        mid = im[:1]
        mids.append(jnp.concatenate([mid * cos_mid, -mid * sin_mid], axis=1))
    pad = -count % 8
    if pad:
        mids.append(jnp.zeros((pad, 2 * N), jnp.float32))
    turned = jnp.concatenate(rows + mids, axis=0)
    spec = mm3(split(turned), (second[0], second[1]))
    spec_re, spec_im = spec[:, :N], spec[:, N:]
    energy = spec_re * spec_re + spec_im * spec_im
    floor = [jnp.broadcast_to(FLOOR * p, (HALF, N)) for p in powers]
    floor += [jnp.broadcast_to(FLOOR * p, (1, N)) for p in powers]
    if pad:
        floor.append(jnp.ones((pad, N), jnp.float32))
    scale = lax.rsqrt(energy + jnp.concatenate(floor, axis=0))
    white = jnp.concatenate([spec_re * scale, spec_im * scale], axis=1)
    back = mm3(split(white), (third[0], third[1]))
    cols = []
    for i in range(count):
        re = back[HALF * i : HALF * (i + 1), :N]
        im = back[HALF * i : HALF * (i + 1), N:]
        mid = HALF * count + i
        mid_re, mid_im = back[mid : mid + 1, :N], back[mid : mid + 1, N:]
        out_re = re * cos - im * sin
        out_im = jnp.where(top, mid_re * cos_mid - mid_im * sin_mid, im * cos + re * sin)
        cols.append(jnp.concatenate([out_re, out_im], axis=0))
    y_hi, y_lo = split(jnp.concatenate(cols, axis=1))
    l_hi, l_lo = last[0], last[1]
    time = mm(jnp.concatenate([l_hi, l_hi], axis=1), jnp.concatenate([y_hi, y_lo], axis=0)) + mm(l_lo, y_hi)
    return [time[:, N * i : N * (i + 1)].T for i in range(count)]


def whiten_kernel(chan_ref, rows_ref, first, second, third, last, turn, win, src_out, chan_out, flat, spec):
    series = []
    flat[...] = chan_ref[:, :BLOCKS].reshape(TM * BLOCKS * 8, N)
    place = lax.broadcasted_iota(jnp.int32, (N, N), 0)
    for c in range(8):
        x = flat[pl.ds(c, N, stride=8), :]
        extra = [jnp.zeros((BLOCKS, N), jnp.float32)]
        for j in range(TM - 1):
            tail = chan_ref[j, SPILL, c : c + 1, :]
            extra.append(jnp.broadcast_to(tail, (BLOCKS, N)))
        extra = jnp.concatenate(extra, axis=0)
        series.append(x + jnp.where(place % BLOCKS == 0, extra, 0.0))
    pieces = []
    for j in range(TM):
        early = rows_ref[0, j, : RS - 1]
        if j > 0:
            tail = rows_ref[1, j - 1, RS - 1 : RS]
            early = early + jnp.where(place[: RS - 1] == 0, tail, 0.0)
        pieces += [early, rows_ref[1, j, : RS - 1]]
    series.append(jnp.concatenate(pieces, axis=0))
    whites = whiten_series(series, first, second, third, last, turn)
    src_out[...] = whites[8]
    data = [jnp.concatenate([w, pltpu.roll(w, N - 1, 1)], axis=0) for w in whites[:8]]
    res = mm3((win[0], win[1]), split(jnp.concatenate(data, axis=1)))
    for i in range(2 * N // 8):
        for c in range(8):
            spec[i, 8 * c : 8 * c + 8] = res[8 * i : 8 * i + 8, N * c : N * (c + 1)]

    def slots(i, carry):
        for k in range(8):
            re = spec[i, pl.ds(k, 8, stride=8), :]
            im = spec[i + N // 8, pl.ds(k, 8, stride=8), :]
            if k == 0:
                single = jnp.broadcast_to(i == 0, re.shape)
                res_re = (re, jnp.where(single, 0.0, im))
                res_im = (jnp.where(single, 0.0, im), jnp.where(single, im, -re))
            else:
                res_re = (re, im)
                res_im = (im, -re)
            whole = []
            for halves in (res_re, res_im):
                for r in range(-LAG_ROWS // 2, LAG_ROWS // 2):
                    moved = [h if r == 0 else pltpu.roll(h, -r % N, 1) for h in halves]
                    whole.append(jnp.concatenate(moved, axis=1))
            hi, lo = split(jnp.concatenate(whole, axis=0))
            chan_out[i * 8 + k] = jnp.concatenate([hi, lo], axis=0)
        return carry

    lax.fori_loop(0, N // 8, slots, 0)


def run_whiten(chan, rows, tables):
    return pl.pallas_call(
        whiten_kernel,
        out_shape=[
            jax.ShapeDtypeStruct((N, N), jnp.float32),
            jax.ShapeDtypeStruct((N, N, 2 * N), jnp.bfloat16),
        ],
        in_specs=[pl.BlockSpec(memory_space=VMEM)] * 8,
        out_specs=[pl.BlockSpec(memory_space=VMEM)] * 2,
        scratch_shapes=[VMEM((TM * BLOCKS * 8, N), jnp.float32), VMEM((2 * N // 8, 64, N), jnp.float32)],
        compiler_params=pltpu.CompilerParams(vmem_limit_bytes=VMEM_LIMIT),
        name="whiten",
    )(chan, rows, *tables)


def gather_kernel(own_ref, out, own_sem, send, recv, f_send, f_recv):
    tm = lax.axis_index("tm")
    ch = lax.axis_index("chan")
    x, zh = tm % 4, tm // 4
    y, zl, core = ch // 4, (ch // 2) % 2, ch % 2
    z = 2 * zh + zl

    def device(axis, d):
        if axis == "x":
            return (zh * 4 + (x + d) % 4, ch)
        if axis == "y":
            return (tm, ((y + d) % 4) * 4 + zl * 2 + core)
        other = (z + d) % 4
        return ((other // 2) * 4 + x, y * 4 + (other % 2) * 2 + core)

    sibling = (tm, ch + 1 - 2 * core)
    peers = [device(axis, d) for axis in "xyz" for d in (1, 2, 3)] + [sibling]
    barrier = pltpu.get_barrier_semaphore()
    for peer in peers:
        pl.semaphore_signal(barrier, inc=1, device_id=peer, device_id_type=MESH)

    mine = pltpu.make_async_copy(own_ref, out.at[y, zl, zh, x], own_sem)
    mine.start()
    mine.wait()
    pl.semaphore_wait(barrier, len(peers))

    def region(kind, phase, d=0):
        start, size, order = KINDS[kind]
        at = {"x": x, "y": y, "z": z}
        axis = order[phase]
        at[axis] = (at[axis] - d) % 4
        done = order[:phase]
        whole = slice(None)
        ix = whole if "x" in done else at["x"]
        iy = whole if "y" in done else at["y"]
        il = whole if "z" in done else at["z"] % 2
        ih = whole if "z" in done else at["z"] // 2
        return out.at[iy, il, ih, ix, pl.ds(core * HALF + start, size)]

    started = []
    for phase in range(3):
        for kind in range(3):
            axis = KINDS[kind][2][phase]
            part = region(kind, phase)
            for d in (1, 3, 2):
                copy = pltpu.make_async_remote_copy(
                    src_ref=part,
                    dst_ref=part,
                    send_sem=send.at[kind, phase, d],
                    recv_sem=recv.at[kind, phase, d],
                    device_id=device(axis, d),
                    device_id_type=MESH,
                )
                copy.start()
                started.append(copy)
        for kind in range(3):
            axis = KINDS[kind][2][phase]
            for d in (1, 3, 2):
                came = region(kind, phase, d)
                pltpu.make_async_remote_copy(
                    src_ref=came,
                    dst_ref=came,
                    send_sem=send.at[kind, phase, d],
                    recv_sem=recv.at[kind, phase, d],
                    device_id=sibling,
                    device_id_type=MESH,
                ).wait_recv()
                copy = pltpu.make_async_remote_copy(
                    src_ref=came,
                    dst_ref=came,
                    send_sem=f_send.at[kind, phase, d],
                    recv_sem=f_recv.at[kind, phase, d],
                    device_id=sibling,
                    device_id_type=MESH,
                )
                copy.start()
                started.append((copy,))
    for copy in started:
        if isinstance(copy, tuple):
            copy[0].wait()
        else:
            copy.wait_send()


def run_gather(own):
    dma = pltpu.SemaphoreType.DMA
    return pl.pallas_call(
        gather_kernel,
        out_shape=jax.ShapeDtypeStruct((4, 2, 2, 4, N, N), jnp.float32),
        in_specs=[pl.BlockSpec(memory_space=VMEM)],
        out_specs=pl.BlockSpec(memory_space=VMEM),
        scratch_shapes=[pltpu.SemaphoreType.DMA] + [dma((3, 3, 4))] * 4,
        compiler_params=pltpu.CompilerParams(collective_id=1, has_side_effects=True, vmem_limit_bytes=VMEM_LIMIT),
        name="gather_sources",
    )(own)


def correlate_kernel(src_ref, chan_ref, win, back, out_ref, spec, prod):
    w_hi, w_lo = win[0][:, :N], win[1][:, :N]
    w_both = jnp.concatenate([w_hi, w_hi], axis=1)

    def transform(g, carry):
        pair = jnp.concatenate([src_ref[2 * g], src_ref[2 * g + 1]], axis=1)
        hi, lo = split(pair)
        res = mm(w_both, jnp.concatenate([hi, lo], axis=0)) + mm(w_lo, hi)
        for i in range(2 * N // 8):
            for e in range(2):
                spec[i, pl.ds(pl.multiple_of((2 * g + e) * 8, 8), 8), :] = res[8 * i : 8 * i + 8, N * e : N * (e + 1)]
        return carry

    lax.fori_loop(0, NSRC // 2, transform, 0)
    left = lax.broadcasted_iota(jnp.int32, (64, N), 1) < HALF

    def slots(i, carry):
        for k in range(8):
            re = spec[i, pl.ds(k, NSRC, stride=8), :]
            im = spec[i + N // 8, pl.ds(k, NSRC, stride=8), :]
            hi, lo = split(jnp.concatenate([re, im], axis=1))
            s_both = jnp.concatenate([hi, lo], axis=0)
            res = lax.dot_general(
                chan_ref[i * 8 + k], s_both, (((1,), (1,)), ((), ())), preferred_element_type=jnp.float32
            )
            u = res[:64] + jnp.where(left, res[64:], 0.0)
            v = u + pltpu.roll(u, HALF, 1)
            prod[pl.ds(pl.multiple_of((i * 8 + k) * 32, 32), 32), :] = jnp.where(left[:32], v[:32], v[32:])
        return carry

    lax.fori_loop(0, N // 8, slots, 0)
    b_hi, b_lo = back[0], back[1]
    for r in range(LAG_ROWS):
        for c in range(8):
            t = prod[pl.ds(r * 8 + c, N, stride=32), :].T
            hi, lo = split(jnp.concatenate([t[:NSRC], t[NSRC:]], axis=1))
            out_ref[c, :, N * r : N * (r + 1)] = mm(hi, b_hi) + mm(hi, b_lo) + mm(lo, b_hi)


def run_correlate(src, chan, win, back):
    return pl.pallas_call(
        correlate_kernel,
        out_shape=jax.ShapeDtypeStruct((8, NSRC, LAG_ROWS * N), jnp.float32),
        in_specs=[pl.BlockSpec(memory_space=VMEM)] * 4,
        out_specs=pl.BlockSpec(memory_space=VMEM),
        scratch_shapes=[VMEM((2 * N // 8, 8 * NSRC, N), jnp.float32), VMEM((N * 32, N), jnp.float32)],
        compiler_params=pltpu.CompilerParams(vmem_limit_bytes=VMEM_LIMIT),
        name="correlate",
    )(src, chan, win, back)


def on_device(strain, fir_taps, source_index):
    first, second, third, last, turn = series_tables()
    win, back = window_tables()
    win = stack_np(win)
    dec, src = run_filter(strain, fir_taps, source_index)
    chan, rows = run_exchange(dec, src)
    own, chan_op = run_whiten(
        chan, rows, (stack_np(first), stack_np(second), stack_np(third), stack_np(last), turn, win)
    )
    sources = run_gather(own).reshape(NSRC, N, N)
    return run_correlate(sources, chan_op, win, stack_np(back))


def solution(mesh):
    return jax.shard_map(
        on_device,
        mesh=mesh,
        in_specs=(P("chan", "tm"), P(), P()),
        out_specs=P(("chan", "tm"), None, None),
        check_vma=False,
    )
```

time: 539 us -> 91.8 us (0.17); the launches traced: 529 us -> 91.6 us
  matrix products: 210 us -> 0 us
  waiting for transfers between devices: 170 us -> 0 us
  other arithmetic: 91.2 us -> 0 us
  Pallas kernels: 0 us -> 90.2 us
  local copies, waits for them, and re-layouts: 31.3 us -> 1.36 us
  between operations: 13.9 us -> 0.02 us
  starting transfers between devices: 11.1 us -> 0 us
    dot_general x56 -> x0, matrix products: 210 us -> none  [the longest x8 54.1 us: correlate(): jnp.einsum('skn,nm->skm', prod_im, cos_p, precision=high)]
    psum x1 -> x0, waiting for transfers between devices: 162 us -> none  [on_device(): src_re, src_im = lax.psum((part_re, part_im), ('tm', 'chan'))]
    pallas_call x0 -> x5, Pallas kernels: none -> 90.2 us  [the longest x1 28.7 us: run_exchange(): pl.pallas_call(exchange_kernel, out_shape=[jax.ShapeDtypeStruct((TM, BLOC...]
    reduce_sum x2 -> x0, other arithmetic: 79.9 us -> none  [filter_blocks(): jnp.sum(padded[:, start:start + count, :] * matrix[offset], axis=-1)]
    while x34 -> x0, local copies, waits for them, and re-layouts: 11.2 us -> none  [the longest x2 11.1 us: on_device(): return lax.map(one_channel, (white_re, white_im))]
    all_to_all x1 -> x0, waiting for transfers between devices: 8.96 us -> none  [on_device(): lax.all_to_all(decimated, 'tm', split_axis=0, concat_axis=1, tiled=True)]
    all_to_all x1 -> x0, starting transfers between devices: 7.15 us -> none  [on_device(): lax.all_to_all(decimated, 'tm', split_axis=0, concat_axis=1, tiled=True)]
    add x2 -> x0, other arithmetic: 5.98 us -> none  [the longest x1 5.97 us: filter_blocks(): total + jnp.sum(padded[:, start:start + count, :] * matrix[offset], axis=-1)]
  transfers between devices with their start and end apart: 3 -> 0, of which waited for: 2 -> 0; matrix products, arithmetic and copies ran while one was open for 1% -> 0% of each run, Pallas kernels for 0% -> 0%
where the time goes in v1:
time: 91.8 us; the launch traced here: 91.6 us
  Pallas kernels  90.2 us (98%)
  local copies, waits for them, and re-layouts  1.36 us (1%)
    pallas_call x1, Pallas kernels, run_exchange(): pl.pallas_call(exchange_kernel, out_shape=[jax.ShapeDtypeStruct((TM, BLOC...  28.7 us
    pallas_call x1, Pallas kernels, run_gather(): pl.pallas_call(gather_kernel, out_shape=jax.ShapeDtypeStruct((4, 2, 2, 4,...  26.8 us
    pallas_call x1, Pallas kernels, run_correlate(): pl.pallas_call(correlate_kernel, out_shape=jax.ShapeDtypeStruct((8, NSRC,...  20.8 us
    pallas_call x1, Pallas kernels, run_whiten(): pl.pallas_call(whiten_kernel, out_shape=[jax.ShapeDtypeStruct((N, N), jnp...  9.58 us
    pallas_call x1, Pallas kernels, run_filter(): pl.pallas_call(filter_kernel, out_shape=[jax.ShapeDtypeStruct((8, BLOCKS...  4.37 us

profile of v1, /device:TPU:1, one launch (start us, length us, event | category | flops | bytes accessed | tf_op | source)
XLA Modules:
  0.0 91.6 jit_solution(16217645373107028100)
XLA Ops:
  0.0 1.4 %copy.11.index_ref = s32[64,1]{1,0:T(8,128)} copy(s32[64,1]{0,1:T(1,128)} %bitcast.3) | data formatting | bytes 512 | tf_op jit(solution)/shard_map/reshape | solution.py:152
  1.4 4.4 %decimate.1 = (f32[8,17,8,128]{3,2,1,0:T(8,128)}, f32[8,17,8,128]{3,2,1,0:T(8,128)}) custom-call(f32[64,8192]{1,0:T(8,128)} %strain_ref.1, f32[64]{0:T(128)} %taps_ref.1, s32[64,1]{1,0:T(8,128)} %copy.11.index_ref), custom_call_target="tpu_custom_call" | custom-call | tf_op jit(solution)/shard_map/decimate/pallas_call | solution.py:140
  5.7 28.7 %exchange.1 = (f32[8,17,8,128]{3,2,1,0:T(8,128)}, f32[2,8,16,128]{3,2,1,0:T(8,128)}) custom-call(f32[8,17,8,128]{3,2,1,0:T(8,128)} %get-tuple-element.11.dec_ref, f32[8,17,8,128]{3,2,1,0:T(8,128)} %get-tuple-element.12.src_ref), custom_call_target="tpu_custom_call" | custom-call | tf_op jit(solution)/shard_map/exchange/pallas_call | solution.py:233
  34.4 9.6 %whiten.1 = (f32[128,128]{1,0:T(8,128)}, bf16[128,128,256]{2,1,0:T(8,128)(2,1)}) custom-call(f32[8,17,8,128]{3,2,1,0:T(8,128)} %get-tuple-element.13.chan_ref, f32[2,8,16,128]{3,2,1,0:T(8,128)} %get-tuple-element.14.rows_ref, bf16[2,128,128]{2,1,0:T(8,128)(2,1)} %constant.14.clone.first, bf16[2,256,256]{2,1,0:T(8,128)(2,1)} %constant.15.clone.second, ...), custom_call_target="tpu_custom_call" | custom-call | tf_op jit(solution)/shard_map/whiten/pallas_call | solution.py:356
  44.0 26.8 %gather_sources.1 = f32[4,2,2,4,128,128]{5,4,3,2,1,0:T(8,128)} custom-call(f32[128,128]{1,0:T(8,128)} %get-tuple-element.15.own_ref), custom_call_target="tpu_custom_call" | custom-call | tf_op jit(solution)/shard_map/gather_sources/pallas_call | solution.py:456
  70.8 20.8 %correlate.1 = f32[8,64,512]{2,1,0:T(8,128)} custom-call(f32[64,128,128]{2,1,0:T(8,128)} %bitcast.2, bf16[128,128,256]{2,1,0:T(8,128)(2,1)} %get-tuple-element.16.chan_ref, bf16[2,256,256]{2,1,0:T(8,128)(2,1)} %constant.19.clone.win, bf16[2,256,128]{2,1,0:T(8,128)(2,1)} %constant.20.clone.back), custom_call_target="tpu_custom_call" | custom-call | tf_op jit(solution)/shard_map/correlate/pallas_call | solution.py:507

commit v2 on v0

v2 whole, which is shorter than its diff:
```python
import functools

import jax
import jax.numpy as jnp
import ml_dtypes
import numpy as np
from jax import lax
from jax.experimental import pallas as pl
from jax.experimental.pallas import tpu as pltpu
from jax.sharding import PartitionSpec as P

MESH = pl.DeviceIdType.MESH
VMEM = pltpu.VMEM
N = 128
NT = N * N
HALF = N // 2
TAPS = 64
NSRC = 64
FLOOR = 0.1
LAG_ROWS = 4
GROUP = 64
TM = 8
BLOCKS = 16
BAND = 5 * N
HB = BLOCKS // 2
PART = HB + 1
KINDS = ((0, 24, "xyz"), (24, 24, "yzx"), (48, 16, "zxy"))
ORDER = (1, 3, 2)
PLANES = (0, 1, 3, 2)
VMEM_LIMIT = 56 * 1024 * 1024


def split_np(table):
    high = table.astype(np.float32).astype(ml_dtypes.bfloat16)
    low = (table - high.astype(np.float64)).astype(np.float32).astype(ml_dtypes.bfloat16)
    return high, low


def stack_np(table):
    return np.stack(split_np(table))


def series_tables():
    k = np.arange(HALF)[:, None]
    q = np.arange(N)[None, :]
    ang = 2 * np.pi * ((k * q) % N) / N
    first = np.concatenate([np.cos(ang), -np.sin(ang)])
    first[HALF] = np.cos(np.pi * np.arange(N))
    ang = 2 * np.pi * ((np.arange(N)[:, None] * np.arange(N)[None, :]) % N) / N
    c, s = np.cos(ang), np.sin(ang)
    second = np.block([[c, -s], [s, c]])
    third = np.block([[c, s], [-s, c]])
    ang = 2 * np.pi * ((np.arange(N)[:, None] * np.arange(HALF)[None, :]) % N) / N
    last = np.concatenate([2 * np.cos(ang), -2 * np.sin(ang)], axis=1) / N
    last[:, 0] = 1.0 / N
    last[:, HALF] = np.cos(np.pi * np.arange(N)) / N
    ang = 2 * np.pi * (np.arange(HALF + 8)[:, None] * np.arange(N)[None, :]) / NT
    turn = np.stack([np.cos(ang), np.sin(ang)]).astype(np.float32)
    return first, second, third, last, turn


def window_tables():
    f = np.arange(N)[:, None]
    u = np.arange(2 * N)[None, :]
    ang = 2 * np.pi * ((f * u) % (2 * N)) / (2 * N)
    win = np.concatenate([np.cos(ang), -np.sin(ang)])
    win[N] = np.cos(np.pi * np.arange(2 * N))
    m = np.arange(N)[None, :]
    ang = 2 * np.pi * ((f * m) % (2 * N)) / (2 * N)
    scale = 1.0 / (2 * N * N)
    back = np.concatenate([2 * np.cos(ang), -2 * np.sin(ang)]) * scale
    back[0] = scale
    back[N] = np.cos(np.pi * np.arange(N)) * scale
    return win, back


def split(value):
    high = value.astype(jnp.bfloat16)
    low = (value - high.astype(jnp.float32)).astype(jnp.bfloat16)
    return high, low


def mm(a, b):
    return jnp.dot(a, b, preferred_element_type=jnp.float32)


def mm3(a, b):
    return mm(a[0], b[0]) + mm(a[0], b[1]) + mm(a[1], b[0])


def whiten_series(series, first, second, third, last, turn):
    count = len(series)
    powers = [jnp.sum(x * x) for x in series]
    x_hi, x_lo = split(jnp.concatenate(series, axis=1))
    a_hi, a_lo = first[0], first[1]
    part = mm(jnp.concatenate([a_hi, a_hi], axis=1), jnp.concatenate([x_hi, x_lo], axis=0)) + mm(a_lo, x_hi)
    cos, sin = turn[0, :HALF], turn[1, :HALF]
    cos_mid, sin_mid = turn[0, HALF : HALF + 1], turn[1, HALF : HALF + 1]
    top = lax.broadcasted_iota(jnp.int32, (HALF, N), 0) == 0
    cos_im = jnp.where(top, 0.0, cos)
    rows, mids = [], []
    for i in range(count):
        re = part[:HALF, N * i : N * (i + 1)]
        im = part[HALF:, N * i : N * (i + 1)]
        rows.append(jnp.concatenate([re * cos + im * sin, im * cos_im - re * sin], axis=1))
        mid = im[:1]
        mids.append(jnp.concatenate([mid * cos_mid, -mid * sin_mid], axis=1))
    pad = -count % 8
    if pad:
        mids.append(jnp.zeros((pad, 2 * N), jnp.float32))
    turned = jnp.concatenate(rows + mids, axis=0)
    spec = mm3(split(turned), (second[0], second[1]))
    spec_re, spec_im = spec[:, :N], spec[:, N:]
    energy = spec_re * spec_re + spec_im * spec_im
    floor = [jnp.broadcast_to(FLOOR * p, (HALF, N)) for p in powers]
    floor += [jnp.broadcast_to(FLOOR * p, (1, N)) for p in powers]
    if pad:
        floor.append(jnp.ones((pad, N), jnp.float32))
    scale = lax.rsqrt(energy + jnp.concatenate(floor, axis=0))
    white = jnp.concatenate([spec_re * scale, spec_im * scale], axis=1)
    back = mm3(split(white), (third[0], third[1]))
    cols = []
    for i in range(count):
        re = back[HALF * i : HALF * (i + 1), :N]
        im = back[HALF * i : HALF * (i + 1), N:]
        mid = HALF * count + i
        mid_re, mid_im = back[mid : mid + 1, :N], back[mid : mid + 1, N:]
        out_re = re * cos - im * sin
        out_im = jnp.where(top, mid_re * cos_mid - mid_im * sin_mid, im * cos + re * sin)
        cols.append(jnp.concatenate([out_re, out_im], axis=0))
    y_hi, y_lo = split(jnp.concatenate(cols, axis=1))
    l_hi, l_lo = last[0], last[1]
    time = mm(jnp.concatenate([l_hi, l_hi], axis=1), jnp.concatenate([y_hi, y_lo], axis=0)) + mm(l_lo, y_hi)
    return [time[:, N * i : N * (i + 1)].T for i in range(count)]


def remote(src, dst, send, recv, device):
    return pltpu.make_async_remote_copy(
        src_ref=src, dst_ref=dst, send_sem=send, recv_sem=recv, device_id=device, device_id_type=MESH
    )


def build_band(taps_ref, band):
    rho = lax.broadcasted_iota(jnp.int32, (8, N), 0)
    lane = lax.broadcasted_iota(jnp.int32, (8, N), 1)
    shifted = 4 * lane - rho
    base = jnp.zeros((8, N), jnp.float32)
    for j in range(TAPS):
        base = jnp.where(shifted == j - 3, taps_ref[j], base)
    for t in range(BAND // 8):
        move = (2 * t - 32) % N
        tap = 4 * lane + (131 - 8 * t) - rho
        rolled = base if move == 0 else pltpu.roll(base, move, 1)
        band[8 * t : 8 * t + 8, :] = jnp.where((tap >= 0) & (tap < TAPS), rolled, 0.0)


def build_picker(index_ref):
    row = lax.broadcasted_iota(jnp.int32, (NSRC, 2 * GROUP), 0)
    wanted = jnp.zeros((NSRC, 2 * GROUP), jnp.int32)
    for s in range(NSRC):
        wanted = jnp.where(row == s, index_ref[s], wanted)
    owned = lax.broadcasted_iota(jnp.int32, (NSRC, 2 * GROUP), 1) % GROUP + lax.axis_index("chan") * GROUP
    return jnp.where(wanted == owned, 1.0, 0.0).astype(jnp.bfloat16)


def kernel(
    strain_hbm, taps_ref, index_ref, first_hbm, second_hbm, third_hbm, last_hbm, turn_hbm, win_hbm, back_hbm, out_ref,
    raw, band, dec, pick, pick_in, total, rs_in, acc, row_buf, rows_in, chan_in, src_all, spec_c, chan_op, spec, prod,
    first, second, third, last, turn, win, back,
    load_sem, own_sem, pick_sem, dec_send, dec_recv, rs_send, rs_recv, row_send, row_recv,
    g_send, g_recv, f_send, f_recv,
):
    tm = lax.axis_index("tm")
    ch = lax.axis_index("chan")
    x, zh = tm % 4, tm // 4
    y, zl, core = ch // 4, (ch // 2) % 2, ch % 2
    z, pair = 2 * zh + zl, ch // 2

    tables = (
        (first_hbm, first), (second_hbm, second), (third_hbm, third), (last_hbm, last), (turn_hbm, turn),
        (win_hbm, win), (back_hbm, back),
    )
    load = pltpu.make_async_copy(strain_hbm, raw.at[:, pl.ds(N, 4 * N * BLOCKS)], load_sem.at[0])
    load.start()
    loads = [pltpu.make_async_copy(a, b, load_sem.at[1 + i]) for i, (a, b) in enumerate(tables)]
    for copy in loads:
        copy.start()

    def device(axis, d):
        if axis == "x":
            return (zh * 4 + (x + d) % 4, ch)
        if axis == "y":
            return (tm, ((y + d) % 4) * 4 + zl * 2 + core)
        other = (z + d) % 4
        return ((other // 2) * 4 + x, y * 4 + (other % 2) * 2 + core)

    sibling = (tm, 2 * pair + 1 - core)
    peers = [sibling]
    peers += [(tm, 2 * ((pair + d) % 8) + core) for d in range(1, 8)]
    peers += [((tm + d) % TM, 2 * pair + (core + e) % 2) for d in range(1, TM) for e in range(2)]
    peers += [((1 - zh) * 4 + x, y * 4 + (1 - zl) * 2 + core)]
    barrier = pltpu.get_barrier_semaphore()
    for peer in peers:
        pl.semaphore_signal(barrier, inc=1, device_id=peer, device_id_type=MESH)

    raw[:, :N] = jnp.zeros((GROUP, N), jnp.float32)
    build_band(taps_ref, band)
    picker = build_picker(index_ref)
    b_hi, b_lo = split(band[...])
    both = jnp.concatenate([b_hi, b_lo], axis=1)
    load.wait()

    def finish(half, block, value):
        for j in range(TM):
            dec[j, half, block] = value[8 * j : 8 * j + 8]
        picked = mm(picker, jnp.concatenate(split(value), axis=0))
        for j in range(NSRC // 8):
            pick[half, j, block] = picked[8 * j : 8 * j + 8]

    hi, lo = split(raw[:, 4 * N * BLOCKS :])
    wide = mm(hi, both[:N])
    finish(1, HB, wide[:, :N] + wide[:, N:] + mm(lo, b_hi[:N]))
    for j in range(TM):
        dec[j, 0, HB] = jnp.zeros((8, N), jnp.float32)
        pick[0, j, HB] = jnp.zeros((8, N), jnp.float32)

    def filter_half(half):
        for b0 in range(0, HB, 4):
            his, los = [], []
            for b in range(b0, b0 + 4):
                start = pl.multiple_of((half * HB + b) * (4 * N), 4 * N)
                hi, lo = split(raw[:, pl.ds(start, BAND)])
                his.append(hi)
                los.append(lo)
            hi, lo = jnp.concatenate(his, axis=0), jnp.concatenate(los, axis=0)
            wide = mm(hi, both)
            value = wide[:, :N] + wide[:, N:] + mm(lo, b_hi)
            for b in range(b0, b0 + 4):
                finish(half, b, value[GROUP * (b - b0) : GROUP * (b - b0 + 1)])

    started = []

    def send_blocks(half, part):
        for d in (1, 3, 2, 4, 5, 7, 6):
            other = (tm + d) % TM
            copy = remote(
                dec.at[other, half], chan_in.at[tm, half], dec_send.at[part, d], dec_recv.at[part, d], (other, ch)
            )
            copy.start()
            started.append(copy)

    filter_half(1 - core)
    pl.semaphore_wait(barrier, len(peers))
    give = remote(pick.at[1 - core], pick_in, pick_sem.at[0], pick_sem.at[1], sibling)
    give.start()
    send_blocks(1 - core, 0)
    filter_half(core)
    own_blocks = pltpu.make_async_copy(dec.at[tm], chan_in.at[tm], own_sem.at[0])
    own_blocks.start()

    give.wait_recv()
    total[...] = pick[core] + pick_in[...]
    sums = []
    for d in (1, 7, 2, 6, 3, 5, 4):
        other = (pair + d) % 8
        copy = remote(total.at[other], rs_in.at[d], rs_send.at[d], rs_recv.at[d], (tm, 2 * other + core))
        copy.start()
        sums.append(copy)
    send_blocks(core, 1)
    for copy in sums:
        copy.wait_recv()
    value = total[pair]
    for d in range(1, 8):
        value = value + rs_in[d]
    acc[...] = value.reshape(PART * 8, N)
    for j in range(TM):
        row_buf[j, :PART] = acc[pl.ds(j, PART, stride=8), :]
        row_buf[j, PART:] = jnp.zeros((16 - PART, N), jnp.float32)
    rows = []
    for d in range(TM):
        for e in range(2):
            if d == 0 and e == 0:
                continue
            other = (tm + d) % TM
            copy = remote(
                row_buf.at[other],
                rows_in.at[core, tm],
                row_send.at[d, e],
                row_recv.at[d, e],
                (other, 2 * pair + (core + e) % 2),
            )
            copy.start()
            rows.append(copy)
    rows_in[core, tm] = row_buf[tm]
    for copy in loads:
        copy.wait()
    for copy in rows:
        copy.wait_recv()
    place = lax.broadcasted_iota(jnp.int32, (HB, N), 0)
    pieces = []
    for j in range(TM):
        early = rows_in[0, j, :HB]
        if j > 0:
            early = early + jnp.where(place == 0, rows_in[1, j - 1, HB : HB + 1], 0.0)
        pieces += [early, rows_in[1, j, :HB]]
    src_all[y, 2 * zl + zh, x] = whiten_series([jnp.concatenate(pieces, axis=0)], first, second, third, last, turn)[0]

    def region(kind, phase, d, plane=None):
        start, size, order = KINDS[kind]
        at = {"x": x, "y": y, "z": z}
        at[order[phase]] = (at[order[phase]] + d) % 4
        done = order[:phase]
        iy = slice(None) if "y" in done else at["y"]
        if plane is not None:
            iy = (y + plane) % 4
        iw = slice(None) if "z" in done else 2 * (at["z"] % 2) + at["z"] // 2
        ix = slice(None) if "x" in done else at["x"]
        return src_all.at[iy, iw, ix, pl.ds(core * HALF + start, size)]

    slots_used = {}

    def slot(*key):
        return slots_used.setdefault(key, len(slots_used))

    def send_part(kind, phase, d, plane=None):
        part = region(kind, phase, 0, plane)
        n = slot(kind, phase, d, plane)
        copy = remote(part, part, g_send.at[n], g_recv.at[n], device(KINDS[kind][2][phase], d))
        copy.start()
        started.append((copy,))

    def pass_on(kind, phase, d, plane=None):
        came = region(kind, phase, -d, plane)
        n = slot(kind, phase, d, plane)
        remote(came, came, g_send.at[n], g_recv.at[n], sibling).wait_recv()
        copy = remote(came, came, f_send.at[n], f_recv.at[n], sibling)
        copy.start()
        started.append((copy,))
        return copy

    for d in ORDER:
        for kind in range(3):
            send_part(kind, 0, d)

    own_blocks.wait()
    for copy in started:
        if not isinstance(copy, tuple):
            copy.wait_recv()

    def channel(c):
        pieces = []
        for j in range(TM):
            for half in range(2):
                value = chan_in[j, half, :HB, c, :]
                if j > 0 and half == 0:
                    value = value + jnp.where(place == 0, chan_in[j - 1, 1, HB, c : c + 1, :], 0.0)
                pieces.append(value)
        return jnp.concatenate(pieces, axis=0)

    def channels(c0):
        whites = whiten_series([channel(c) for c in range(c0, c0 + 4)], first, second, third, last, turn)
        data = [jnp.concatenate([w, pltpu.roll(w, N - 1, 1)], axis=0) for w in whites]
        res = mm3((win[0], win[1]), split(jnp.concatenate(data, axis=1)))
        for i in range(2 * N // 8):
            for c in range(4):
                at = 8 * (c0 + c)
                spec_c[i, at : at + 8] = res[8 * i : 8 * i + 8, N * c : N * (c + 1)]

    channels(0)
    forwards = []
    for d in ORDER:
        for kind in range(3):
            forwards.append(pass_on(kind, 0, d))
    for d in ORDER:
        for kind in range(3):
            send_part(kind, 1, d)
    channels(4)
    for d in ORDER:
        for kind in range(3):
            forwards.append(pass_on(kind, 1, d))
    for d in ORDER:
        send_part(2, 2, d)
        for kind in range(2):
            send_part(kind, 2, d, 0)
    for plane in PLANES[1:]:
        for d in ORDER:
            for kind in range(2):
                send_part(kind, 2, d, plane)

    def channel_slots(i, carry):
        for k in range(8):
            re = spec_c[i, pl.ds(k, 8, stride=8), :]
            im = spec_c[i + N // 8, pl.ds(k, 8, stride=8), :]
            if k == 0:
                single = jnp.broadcast_to(i == 0, re.shape)
                res_re = (re, jnp.where(single, 0.0, im))
                res_im = (jnp.where(single, 0.0, im), jnp.where(single, im, -re))
            else:
                res_re = (re, im)
                res_im = (im, -re)
            whole = []
            for halves in (res_re, res_im):
                for r in range(-LAG_ROWS // 2, LAG_ROWS // 2):
                    moved = [h if r == 0 else pltpu.roll(h, -r % N, 1) for h in halves]
                    whole.append(jnp.concatenate(moved, axis=1))
            hi, lo = split(jnp.concatenate(whole, axis=0))
            chan_op[i * 8 + k] = jnp.concatenate([hi, lo], axis=0)
        return carry

    lax.fori_loop(0, N // 8, channel_slots, 0)

    w_hi, w_lo = win[0][:, :N], win[1][:, :N]
    w_both = jnp.concatenate([w_hi, w_hi], axis=1)

    def transform(at_y):
        def four(g, carry):
            hi, lo = split(jnp.concatenate([src_all[at_y, g, e] for e in range(4)], axis=1))
            res = mm(w_both, jnp.concatenate([hi, lo], axis=0)) + mm(w_lo, hi)
            for i in range(2 * N // 8):
                for e in range(4):
                    at = pl.multiple_of(((at_y * 4 + g) * 4 + e) * 8, 8)
                    spec[i, pl.ds(at, 8), :] = res[8 * i : 8 * i + 8, N * e : N * (e + 1)]
            return carry

        lax.fori_loop(0, 4, four, 0)

    for plane in PLANES:
        if plane:
            forwards.append(pass_on(2, 2, (-plane) % 4))
        for d in ORDER:
            for kind in range(2):
                forwards.append(pass_on(kind, 2, d, plane))
        for copy in forwards:
            copy.wait_recv()
        forwards = []
        transform((y + plane) % 4)

    left = lax.broadcasted_iota(jnp.int32, (64, N), 1) < HALF

    def slots(i, carry):
        for k in range(8):
            re = spec[i, pl.ds(k, NSRC, stride=8), :]
            im = spec[i + N // 8, pl.ds(k, NSRC, stride=8), :]
            hi, lo = split(jnp.concatenate([re, im], axis=1))
            res = lax.dot_general(
                chan_op[i * 8 + k],
                jnp.concatenate([hi, lo], axis=0),
                (((1,), (1,)), ((), ())),
                preferred_element_type=jnp.float32,
            )
            u = res[:64] + jnp.where(left, res[64:], 0.0)
            v = u + pltpu.roll(u, HALF, 1)
            prod[pl.ds(pl.multiple_of((i * 8 + k) * 32, 32), 32), :] = jnp.where(left[:32], v[:32], v[32:])
        return carry

    lax.fori_loop(0, N // 8, slots, 0)
    k_hi, k_lo = back[0], back[1]
    for r in range(LAG_ROWS):
        for c in range(8):
            t = prod[pl.ds(r * 8 + c, N, stride=32), :].T
            hi, lo = split(jnp.concatenate([t[:NSRC], t[NSRC:]], axis=1))
            out_ref[c, :, N * r : N * (r + 1)] = mm(hi, k_hi) + mm(hi, k_lo) + mm(lo, k_hi)

    give.wait_send()
    for copy in sums + rows:
        copy.wait_send()
    for copy in started:
        (copy[0] if isinstance(copy, tuple) else copy).wait_send()


def on_device(strain, fir_taps, source_index):
    tables = series_tables()
    win, back = window_tables()
    tables = [stack_np(t) for t in tables[:4]] + [tables[4], stack_np(win), stack_np(back)]
    dma = pltpu.SemaphoreType.DMA
    f32 = jnp.float32
    smem = pl.BlockSpec(memory_space=pltpu.SMEM)
    anywhere = pl.BlockSpec(memory_space=pl.ANY)
    return pl.pallas_call(
        kernel,
        out_shape=jax.ShapeDtypeStruct((8, NSRC, LAG_ROWS * N), f32),
        in_specs=[anywhere, smem, smem] + [anywhere] * len(tables),
        out_specs=pl.BlockSpec(memory_space=VMEM),
        scratch_shapes=[
            VMEM((GROUP, N + 4 * N * BLOCKS), f32),
            VMEM((BAND, N), f32),
            VMEM((TM, 2, PART, 8, N), f32),
            VMEM((2, 8, PART, 8, N), f32),
            VMEM((8, PART, 8, N), f32),
            VMEM((8, PART, 8, N), f32),
            VMEM((8, PART, 8, N), f32),
            VMEM((PART * 8, N), f32),
            VMEM((TM, 16, N), f32),
            VMEM((2, TM, 16, N), f32),
            VMEM((TM, 2, PART, 8, N), f32),
            VMEM((4, 4, 4, N, N), f32),
            VMEM((2 * N // 8, 64, N), f32),
            VMEM((N, N, 2 * N), jnp.bfloat16),
            VMEM((2 * N // 8, 8 * NSRC, N), f32),
            VMEM((N * 32, N), f32),
        ]
        + [VMEM(t.shape, jnp.dtype(t.dtype)) for t in tables]
        + [
            dma((1 + len(tables),)),
            dma((1,)),
            dma((2,)),
            dma((2, TM)),
            dma((2, TM)),
            dma((8,)),
            dma((8,)),
            dma((TM, 2)),
            dma((TM, 2)),
        ]
        + [dma((48,))] * 4,
        compiler_params=pltpu.CompilerParams(
            collective_id=0, has_side_effects=True, vmem_limit_bytes=VMEM_LIMIT
        ),
        name="interferometry",
    )(strain, fir_taps, source_index, *tables)


def solution(mesh):
    return jax.shard_map(
        on_device,
        mesh=mesh,
        in_specs=(P("chan", "tm"), P(), P()),
        out_specs=P(("chan", "tm"), None, None),
        check_vma=False,
    )
```

time: 539 us -> 64.7 us (0.12); the launches traced: 529 us -> 64.5 us
  matrix products: 210 us -> 0 us
  waiting for transfers between devices: 170 us -> 0 us
  other arithmetic: 91.2 us -> 0 us
  Pallas kernels: 0 us -> 62.2 us
  local copies, waits for them, and re-layouts: 31.3 us -> 2.26 us
  between operations: 13.9 us -> 0.01 us
  starting transfers between devices: 11.1 us -> 0 us
    dot_general x56 -> x0, matrix products: 210 us -> none  [the longest x8 54.1 us: correlate(): jnp.einsum('skn,nm->skm', prod_im, cos_p, precision=high)]
    psum x1 -> x0, waiting for transfers between devices: 162 us -> none  [on_device(): src_re, src_im = lax.psum((part_re, part_im), ('tm', 'chan'))]
    reduce_sum x2 -> x0, other arithmetic: 79.9 us -> none  [filter_blocks(): jnp.sum(padded[:, start:start + count, :] * matrix[offset], axis=-1)]
    pallas_call x0 -> x1, Pallas kernels: none -> 62.2 us  [on_device(): pl.pallas_call(kernel, out_shape=jax.ShapeDtypeStruct((8, NSRC, LAG_ROWS...]
    while x34 -> x0, local copies, waits for them, and re-layouts: 11.2 us -> none  [the longest x2 11.1 us: on_device(): return lax.map(one_channel, (white_re, white_im))]
    all_to_all x1 -> x0, waiting for transfers between devices: 8.96 us -> none  [on_device(): lax.all_to_all(decimated, 'tm', split_axis=0, concat_axis=1, tiled=True)]
    all_to_all x1 -> x0, starting transfers between devices: 7.15 us -> none  [on_device(): lax.all_to_all(decimated, 'tm', split_axis=0, concat_axis=1, tiled=True)]
    add x2 -> x0, other arithmetic: 5.98 us -> none  [the longest x1 5.97 us: filter_blocks(): total + jnp.sum(padded[:, start:start + count, :] * matrix[offset], axis=-1)]
  transfers between devices with their start and end apart: 3 -> 0, of which waited for: 2 -> 0; matrix products, arithmetic and copies ran while one was open for 1% -> 0% of each run, Pallas kernels for 0% -> 0%
where the time goes in v2:
time: 64.7 us; the launch traced here: 64.5 us
  Pallas kernels  62.2 us (96%)
  local copies, waits for them, and re-layouts  2.26 us (3%)
    pallas_call x1, Pallas kernels, on_device(): pl.pallas_call(kernel, out_shape=jax.ShapeDtypeStruct((8, NSRC, LAG_ROWS...  62.2 us
    unnamed x1, local copies, waits for them, and re-layouts  2.26 us

profile of v2, /device:TPU:1, one launch (start us, length us, event | category | flops | bytes accessed | tf_op | source)
XLA Modules:
  0.0 64.5 jit_solution(9178801844271572623)
XLA Ops:
  0.0 62.2 %interferometry.1 = f32[8,64,512]{2,1,0:T(8,128)} custom-call(f32[64,8192]{1,0:T(8,128)} %strain_hbm.1, f32[64]{0:T(128)} %taps_ref.1, s32[64]{0:T(128)} %index_ref.1, bf16[2,128,128]{2,1,0:T(8,128)(2,1)} %constant.14.clone.first_hbm, bf16[2,256,256]{2,1,0:T(8,128)(2,1)} %constant.15.clone.second_hbm, bf16[2,256,256]{2,1,0:T(8,128)(2,1)} %constant.16.clone.third_hbm, ...), custom_call_target="tpu_custom_call" | custom-call | tf_op jit(solution)/shard_map/interferometry/pallas_call | solution.py:479
  62.3 2.3 %copy.12 = f32[8,64,512]{2,1,0:T(8,128)} copy(f32[8,64,512]{2,1,0:T(8,128)} %interferometry.1) | data formatting | bytes 2097152

commit v3 on v2

--- a/solution.py
+++ b/solution.py
@@ -26,7 +26,7 @@
 PART = HB + 1
 KINDS = ((0, 24, "xyz"), (24, 24, "yzx"), (48, 16, "zxy"))
 ORDER = (1, 3, 2)
-PLANES = (0, 1, 3, 2)
+UNROLL = 32
 VMEM_LIMIT = 56 * 1024 * 1024
 
 
@@ -212,7 +212,7 @@
 
     def finish(half, block, value):
         for j in range(TM):
-            dec[j, half, block] = value[8 * j : 8 * j + 8]
+            dec[j, half * HB + block] = value[8 * j : 8 * j + 8]
         picked = mm(picker, jnp.concatenate(split(value), axis=0))
         for j in range(NSRC // 8):
             pick[half, j, block] = picked[8 * j : 8 * j + 8]
@@ -220,8 +220,7 @@
     hi, lo = split(raw[:, 4 * N * BLOCKS :])
     wide = mm(hi, both[:N])
     finish(1, HB, wide[:, :N] + wide[:, N:] + mm(lo, b_hi[:N]))
-    for j in range(TM):
-        dec[j, 0, HB] = jnp.zeros((8, N), jnp.float32)
+    for j in range(NSRC // 8):
         pick[0, j, HB] = jnp.zeros((8, N), jnp.float32)
 
     def filter_half(half):
@@ -240,20 +239,10 @@
 
     started = []
 
-    def send_blocks(half, part):
-        for d in (1, 3, 2, 4, 5, 7, 6):
-            other = (tm + d) % TM
-            copy = remote(
-                dec.at[other, half], chan_in.at[tm, half], dec_send.at[part, d], dec_recv.at[part, d], (other, ch)
-            )
-            copy.start()
-            started.append(copy)
-
     filter_half(1 - core)
     pl.semaphore_wait(barrier, len(peers))
     give = remote(pick.at[1 - core], pick_in, pick_sem.at[0], pick_sem.at[1], sibling)
     give.start()
-    send_blocks(1 - core, 0)
     filter_half(core)
     own_blocks = pltpu.make_async_copy(dec.at[tm], chan_in.at[tm], own_sem.at[0])
     own_blocks.start()
@@ -266,7 +255,6 @@
         copy = remote(total.at[other], rs_in.at[d], rs_send.at[d], rs_recv.at[d], (tm, 2 * other + core))
         copy.start()
         sums.append(copy)
-    send_blocks(core, 1)
     for copy in sums:
         copy.wait_recv()
     value = total[pair]
@@ -292,6 +280,12 @@
             copy.start()
             rows.append(copy)
     rows_in[core, tm] = row_buf[tm]
+    blocks = []
+    for d in (1, 3, 2, 4, 5, 7, 6):
+        other = (tm + d) % TM
+        copy = remote(dec.at[other], chan_in.at[tm], dec_send.at[d], dec_recv.at[d], (other, ch))
+        copy.start()
+        blocks.append(copy)
     for copy in loads:
         copy.wait()
     for copy in rows:
@@ -303,58 +297,71 @@
         if j > 0:
             early = early + jnp.where(place == 0, rows_in[1, j - 1, HB : HB + 1], 0.0)
         pieces += [early, rows_in[1, j, :HB]]
-    src_all[y, 2 * zl + zh, x] = whiten_series([jnp.concatenate(pieces, axis=0)], first, second, third, last, turn)[0]
-
-    def region(kind, phase, d, plane=None):
+    src_all[0, 0, 0] = whiten_series([jnp.concatenate(pieces, axis=0)], first, second, third, last, turn)[0]
+
+    REST = pl.ds(1, 3)
+
+    def region(kind, offsets):
         start, size, order = KINDS[kind]
-        at = {"x": x, "y": y, "z": z}
-        at[order[phase]] = (at[order[phase]] + d) % 4
-        done = order[:phase]
-        iy = slice(None) if "y" in done else at["y"]
-        if plane is not None:
-            iy = (y + plane) % 4
-        iw = slice(None) if "z" in done else 2 * (at["z"] % 2) + at["z"] // 2
-        ix = slice(None) if "x" in done else at["x"]
-        return src_all.at[iy, iw, ix, pl.ds(core * HALF + start, size)]
-
-    slots_used = {}
-
-    def slot(*key):
-        return slots_used.setdefault(key, len(slots_used))
-
-    def send_part(kind, phase, d, plane=None):
-        part = region(kind, phase, 0, plane)
-        n = slot(kind, phase, d, plane)
-        copy = remote(part, part, g_send.at[n], g_recv.at[n], device(KINDS[kind][2][phase], d))
+        at = dict(zip(order, offsets))
+        return src_all.at[at["y"], at["z"], at["x"], pl.ds(core * HALF + start, size)]
+
+    counts = [{}, {}]
+
+    def number(which, key):
+        return counts[which].setdefault(key, len(counts[which]))
+
+    def placed(offsets, axis, d):
+        return tuple((4 - d) if i == axis else o for i, o in enumerate(offsets))
+
+    def tag(offsets):
+        return tuple("*" if not isinstance(o, int) else o for o in offsets)
+
+    def send_on(kind, offsets, axis):
+        for d in ORDER:
+            to = placed(offsets, axis, d)
+            n = number(0, (kind, tag(to), axis))
+            copy = remote(
+                region(kind, offsets), region(kind, to), g_send.at[n], g_recv.at[n], device(KINDS[kind][2][axis], d)
+            )
+            copy.start()
+            started.append(copy)
+
+    def arrived(kind, offsets, axis, ds=ORDER):
+        for d in ds:
+            to = placed(offsets, axis, d)
+            n = number(0, (kind, tag(to), axis))
+            part = region(kind, to)
+            remote(part, part, g_send.at[n], g_recv.at[n], sibling).wait_recv()
+
+    def share(kind, offsets):
+        part = region(kind, offsets)
+        n = number(1, (kind, tag(offsets)))
+        copy = remote(part, part, f_send.at[n], f_recv.at[n], sibling)
         copy.start()
-        started.append((copy,))
-
-    def pass_on(kind, phase, d, plane=None):
-        came = region(kind, phase, -d, plane)
-        n = slot(kind, phase, d, plane)
-        remote(came, came, g_send.at[n], g_recv.at[n], sibling).wait_recv()
-        copy = remote(came, came, f_send.at[n], f_recv.at[n], sibling)
-        copy.start()
-        started.append((copy,))
-        return copy
-
-    for d in ORDER:
-        for kind in range(3):
-            send_part(kind, 0, d)
-
-    own_blocks.wait()
-    for copy in started:
-        if not isinstance(copy, tuple):
+        started.append(copy)
+        shared.append(copy)
+
+    def settle():
+        for copy in shared:
             copy.wait_recv()
+        shared.clear()
+
+    shared = []
+    kinds = range(3)
+    for axis in range(3):
+        for kind in kinds:
+            send_on(kind, (0, 0, 0), axis)
+
+    place = lax.broadcasted_iota(jnp.int32, (BLOCKS, N), 0)
 
     def channel(c):
         pieces = []
         for j in range(TM):
-            for half in range(2):
-                value = chan_in[j, half, :HB, c, :]
-                if j > 0 and half == 0:
-                    value = value + jnp.where(place == 0, chan_in[j - 1, 1, HB, c : c + 1, :], 0.0)
-                pieces.append(value)
+            value = chan_in[j, :BLOCKS, c, :]
+            if j > 0:
+                value = value + jnp.where(place == 0, chan_in[j - 1, BLOCKS, c : c + 1, :], 0.0)
+            pieces.append(value)
         return jnp.concatenate(pieces, axis=0)
 
     def channels(c0):
@@ -366,40 +373,17 @@
                 at = 8 * (c0 + c)
                 spec_c[i, at : at + 8] = res[8 * i : 8 * i + 8, N * c : N * (c + 1)]
 
-    channels(0)
-    forwards = []
-    for d in ORDER:
-        for kind in range(3):
-            forwards.append(pass_on(kind, 0, d))
-    for d in ORDER:
-        for kind in range(3):
-            send_part(kind, 1, d)
-    channels(4)
-    for d in ORDER:
-        for kind in range(3):
-            forwards.append(pass_on(kind, 1, d))
-    for d in ORDER:
-        send_part(2, 2, d)
-        for kind in range(2):
-            send_part(kind, 2, d, 0)
-    for plane in PLANES[1:]:
-        for d in ORDER:
-            for kind in range(2):
-                send_part(kind, 2, d, plane)
-
     def channel_slots(i, carry):
         for k in range(8):
             re = spec_c[i, pl.ds(k, 8, stride=8), :]
             im = spec_c[i + N // 8, pl.ds(k, 8, stride=8), :]
+            straight, crossed = (re, im), (im, -re)
             if k == 0:
                 single = jnp.broadcast_to(i == 0, re.shape)
-                res_re = (re, jnp.where(single, 0.0, im))
-                res_im = (jnp.where(single, 0.0, im), jnp.where(single, im, -re))
-            else:
-                res_re = (re, im)
-                res_im = (im, -re)
+                straight = (re, jnp.where(single, 0.0, im))
+                crossed = (jnp.where(single, 0.0, im), jnp.where(single, im, -re))
             whole = []
-            for halves in (res_re, res_im):
+            for halves in (straight, crossed):
                 for r in range(-LAG_ROWS // 2, LAG_ROWS // 2):
                     moved = [h if r == 0 else pltpu.roll(h, -r % N, 1) for h in halves]
                     whole.append(jnp.concatenate(moved, axis=1))
@@ -407,65 +391,107 @@
             chan_op[i * 8 + k] = jnp.concatenate([hi, lo], axis=0)
         return carry
 
+    for kind in kinds:
+        arrived(kind, (0, 0, 0), 0)
+        send_on(kind, (REST, 0, 0), 1)
+        share(kind, (REST, 0, 0))
+    for kind in kinds:
+        arrived(kind, (0, 0, 0), 1)
+        send_on(kind, (REST, 0, 0), 2)
+        send_on(kind, (0, REST, 0), 2)
+        share(kind, (0, REST, 0))
+    for kind in kinds:
+        arrived(kind, (0, 0, 0), 2)
+        share(kind, (0, 0, REST))
+    own_blocks.wait()
+    for copy in blocks:
+        copy.wait_recv()
+    channels(0)
+    for kind in kinds:
+        arrived(kind, (REST, 0, 0), 1)
+        send_on(kind, (REST, REST, 0), 2)
+        share(kind, (REST, REST, 0))
+    channels(4)
     lax.fori_loop(0, N // 8, channel_slots, 0)
+    for kind in kinds:
+        arrived(kind, (REST, 0, 0), 2)
+        share(kind, (REST, 0, REST))
+        arrived(kind, (0, REST, 0), 2)
+        share(kind, (0, REST, REST))
+    settle()
 
     w_hi, w_lo = win[0][:, :N], win[1][:, :N]
     w_both = jnp.concatenate([w_hi, w_hi], axis=1)
 
-    def transform(at_y):
-        def four(g, carry):
-            hi, lo = split(jnp.concatenate([src_all[at_y, g, e] for e in range(4)], axis=1))
-            res = mm(w_both, jnp.concatenate([hi, lo], axis=0)) + mm(w_lo, hi)
-            for i in range(2 * N // 8):
-                for e in range(4):
-                    at = pl.multiple_of(((at_y * 4 + g) * 4 + e) * 8, 8)
-                    spec[i, pl.ds(at, 8), :] = res[8 * i : 8 * i + 8, N * e : N * (e + 1)]
-            return carry
-
-        lax.fori_loop(0, 4, four, 0)
-
-    for plane in PLANES:
-        if plane:
-            forwards.append(pass_on(2, 2, (-plane) % 4))
-        for d in ORDER:
-            for kind in range(2):
-                forwards.append(pass_on(kind, 2, d, plane))
-        for copy in forwards:
-            copy.wait_recv()
-        forwards = []
-        transform((y + plane) % 4)
-
-    left = lax.broadcasted_iota(jnp.int32, (64, N), 1) < HALF
+    def transform(places):
+        hi, lo = split(jnp.concatenate([src_all[ry, rz, rx] for ry, rz, rx in places], axis=1))
+        rows = []
+        for ry, rz, rx in places:
+            z_s = (z + rz) % 4
+            source = 8 * (2 * ((y + ry) % 4) + z_s % 2) + 4 * (z_s // 2) + (x + rx) % 4
+            rows.append(pl.ds(pl.multiple_of(source * 8, 8), 8))
+        res = mm(w_both, jnp.concatenate([hi, lo], axis=0)) + mm(w_lo, hi)
+        for i in range(2 * N // 8):
+            for e, at in enumerate(rows):
+                spec[i, at, :] = res[8 * i : 8 * i + 8, N * e : N * (e + 1)]
+
+    def column(ry, carry):
+        transform([(ry, rz, 0) for rz in range(4)])
+        return carry
+
+    def early(t, carry):
+        ry = jnp.where(t < 4, t, 0)
+        rz = jnp.where(t < 4, 0, t - 3)
+        transform([(ry, rz, rx) for rx in range(1, 4)])
+        return carry
+
+    def late(ry, carry):
+        transform([(ry, rz, rx) for rz in range(1, 4) for rx in range(1, 4)])
+        return carry
+
+    lax.fori_loop(0, 4, column, 0)
+    lax.fori_loop(0, 7, early, 0)
+
+    left = lax.broadcasted_iota(jnp.int32, (NSRC, N), 1) < HALF
 
     def slots(i, carry):
-        for k in range(8):
-            re = spec[i, pl.ds(k, NSRC, stride=8), :]
-            im = spec[i + N // 8, pl.ds(k, NSRC, stride=8), :]
+        for k in range(UNROLL):
+            n = i * UNROLL + k
+            tile = i * (UNROLL // 8) + k // 8
+            re = spec[tile, pl.ds(k % 8, NSRC, stride=8), :]
+            im = spec[tile + N // 8, pl.ds(k % 8, NSRC, stride=8), :]
             hi, lo = split(jnp.concatenate([re, im], axis=1))
             res = lax.dot_general(
-                chan_op[i * 8 + k],
+                chan_op[n],
                 jnp.concatenate([hi, lo], axis=0),
                 (((1,), (1,)), ((), ())),
                 preferred_element_type=jnp.float32,
             )
             u = res[:64] + jnp.where(left, res[64:], 0.0)
             v = u + pltpu.roll(u, HALF, 1)
-            prod[pl.ds(pl.multiple_of((i * 8 + k) * 32, 32), 32), :] = jnp.where(left[:32], v[:32], v[32:])
+            prod[pl.ds(pl.multiple_of(n * 32, 32), 32), :] = jnp.where(left[:32], v[:32], v[32:])
         return carry
 
-    lax.fori_loop(0, N // 8, slots, 0)
-    k_hi, k_lo = back[0], back[1]
+    for kind in kinds:
+        for d in ORDER:
+            arrived(kind, (REST, REST, 0), 2, (d,))
+            share(kind, (REST, REST, 4 - d))
+    settle()
+    lax.fori_loop(1, 4, late, 0)
+    lax.fori_loop(0, N // UNROLL, slots, 0)
+
+    k_hi = back[0]
+    k_both = jnp.concatenate([back[0], back[1]], axis=1)
     for r in range(LAG_ROWS):
         for c in range(8):
             t = prod[pl.ds(r * 8 + c, N, stride=32), :].T
             hi, lo = split(jnp.concatenate([t[:NSRC], t[NSRC:]], axis=1))
-            out_ref[c, :, N * r : N * (r + 1)] = mm(hi, k_hi) + mm(hi, k_lo) + mm(lo, k_hi)
+            wide = mm(hi, k_both)
+            out_ref[c, :, N * r : N * (r + 1)] = wide[:, :N] + wide[:, N:] + mm(lo, k_hi)
 
     give.wait_send()
-    for copy in sums + rows:
+    for copy in sums + rows + blocks + started:
         copy.wait_send()
-    for copy in started:
-        (copy[0] if isinstance(copy, tuple) else copy).wait_send()
 
 
 def on_device(strain, fir_taps, source_index):
@@ -484,7 +510,7 @@
         scratch_shapes=[
             VMEM((GROUP, N + 4 * N * BLOCKS), f32),
             VMEM((BAND, N), f32),
-            VMEM((TM, 2, PART, 8, N), f32),
+            VMEM((TM, BLOCKS + 1, 8, N), f32),
             VMEM((2, 8, PART, 8, N), f32),
             VMEM((8, PART, 8, N), f32),
             VMEM((8, PART, 8, N), f32),
@@ -492,7 +518,7 @@
             VMEM((PART * 8, N), f32),
             VMEM((TM, 16, N), f32),
             VMEM((2, TM, 16, N), f32),
-            VMEM((TM, 2, PART, 8, N), f32),
+            VMEM((TM, BLOCKS + 1, 8, N), f32),
             VMEM((4, 4, 4, N, N), f32),
             VMEM((2 * N // 8, 64, N), f32),
             VMEM((N, N, 2 * N), jnp.bfloat16),
@@ -504,14 +530,15 @@
             dma((1 + len(tables),)),
             dma((1,)),
             dma((2,)),
-            dma((2, TM)),
-            dma((2, TM)),
+            dma((TM,)),
+            dma((TM,)),
             dma((8,)),
             dma((8,)),
             dma((TM, 2)),
             dma((TM, 2)),
         ]
-        + [dma((48,))] * 4,
+        + [dma((81,))] * 2
+        + [dma((27,))] * 2,
         compiler_params=pltpu.CompilerParams(
             collective_id=0, has_side_effects=True, vmem_limit_bytes=VMEM_LIMIT
         ),

time: 64.7 us -> 58.2 us (0.90)
  Pallas kernels: 62.2 us -> 55.3 us
    pallas_call x1, Pallas kernels: 62.2 us -> 55.3 us  [on_device(): pl.pallas_call(kernel, out_shape=jax.ShapeDtypeStruct((8, NSRC, LAG_ROWS...]
where the time goes in v3:
time: 58.2 us; the launch traced here: 57.5 us
  Pallas kernels  55.3 us (95%)
  local copies, waits for them, and re-layouts  2.26 us (4%)
    pallas_call x1, Pallas kernels, on_device(): pl.pallas_call(kernel, out_shape=jax.ShapeDtypeStruct((8, NSRC, LAG_ROWS...  55.3 us
    unnamed x1, local copies, waits for them, and re-layouts  2.26 us

profile of v3, /device:TPU:1, one launch (start us, length us, event | category | flops | bytes accessed | tf_op | source)
XLA Modules:
  0.0 57.5 jit_solution(7489330001881553438)
XLA Ops:
  0.0 55.3 %interferometry.1 = f32[8,64,512]{2,1,0:T(8,128)} custom-call(f32[64,8192]{1,0:T(8,128)} %strain_hbm.1, f32[64]{0:T(128)} %taps_ref.1, s32[64]{0:T(128)} %index_ref.1, bf16[2,128,128]{2,1,0:T(8,128)(2,1)} %constant.14.clone.first_hbm, bf16[2,256,256]{2,1,0:T(8,128)(2,1)} %constant.15.clone.second_hbm, bf16[2,256,256]{2,1,0:T(8,128)(2,1)} %constant.16.clone.third_hbm, ...), custom_call_target="tpu_custom_call" | custom-call | tf_op jit(solution)/shard_map/interferometry/pallas_call | solution.py:505
  55.3 2.3 %copy.12 = f32[8,64,512]{2,1,0:T(8,128)} copy(f32[8,64,512]{2,1,0:T(8,128)} %interferometry.1) | data formatting | bytes 2097152

commit v4 on v3

--- a/solution.py
+++ b/solution.py
@@ -26,7 +26,7 @@
 PART = HB + 1
 KINDS = ((0, 24, "xyz"), (24, 24, "yzx"), (48, 16, "zxy"))
 ORDER = (1, 3, 2)
-UNROLL = 32
+UNROLL = 64
 VMEM_LIMIT = 56 * 1024 * 1024
 
 
@@ -164,11 +164,11 @@
 
 
 def kernel(
-    strain_hbm, taps_ref, index_ref, first_hbm, second_hbm, third_hbm, last_hbm, turn_hbm, win_hbm, back_hbm, out_ref,
-    raw, band, dec, pick, pick_in, total, rs_in, acc, row_buf, rows_in, chan_in, src_all, spec_c, chan_op, spec, prod,
-    first, second, third, last, turn, win, back,
+    strain_hbm, taps_ref, index_ref, first_hbm, second_hbm, third_hbm, last_hbm, turn_hbm, win_hbm, out_hbm,
+    raw, band, dec, pick, pick_in, total, rs_in, acc, row_buf, rows_in, halves, chan_in, src_all, spec_c, chan_op, spec, prod,
+    first, second, third, last, turn, win,
     load_sem, own_sem, pick_sem, dec_send, dec_recv, rs_send, rs_recv, row_send, row_recv,
-    g_send, g_recv, f_send, f_recv,
+    g_send, g_recv, f_send, f_recv, out_sem,
 ):
     tm = lax.axis_index("tm")
     ch = lax.axis_index("chan")
@@ -178,7 +178,7 @@
 
     tables = (
         (first_hbm, first), (second_hbm, second), (third_hbm, third), (last_hbm, last), (turn_hbm, turn),
-        (win_hbm, win), (back_hbm, back),
+        (win_hbm, win),
     )
     load = pltpu.make_async_copy(strain_hbm, raw.at[:, pl.ds(N, 4 * N * BLOCKS)], load_sem.at[0])
     load.start()
@@ -195,10 +195,14 @@
         return ((other // 2) * 4 + x, y * 4 + (other % 2) * 2 + core)
 
     sibling = (tm, 2 * pair + 1 - core)
+    plane = 8 * zl + tm
+
+    def in_plane(n):
+        return (n % TM, 4 * y + 2 * (n // TM) + core)
+
     peers = [sibling]
-    peers += [(tm, 2 * ((pair + d) % 8) + core) for d in range(1, 8)]
-    peers += [((tm + d) % TM, 2 * pair + (core + e) % 2) for d in range(1, TM) for e in range(2)]
-    peers += [((1 - zh) * 4 + x, y * 4 + (1 - zl) * 2 + core)]
+    peers += [device("y", d) for d in ORDER]
+    peers += [in_plane((plane + d) % 16) for d in range(1, 16)]
     barrier = pltpu.get_barrier_semaphore()
     for peer in peers:
         pl.semaphore_signal(barrier, inc=1, device_id=peer, device_id_type=MESH)
@@ -247,56 +251,49 @@
     own_blocks = pltpu.make_async_copy(dec.at[tm], chan_in.at[tm], own_sem.at[0])
     own_blocks.start()
 
-    give.wait_recv()
-    total[...] = pick[core] + pick_in[...]
-    sums = []
-    for d in (1, 7, 2, 6, 3, 5, 4):
-        other = (pair + d) % 8
-        copy = remote(total.at[other], rs_in.at[d], rs_send.at[d], rs_recv.at[d], (tm, 2 * other + core))
-        copy.start()
-        sums.append(copy)
-    for copy in sums:
-        copy.wait_recv()
-    value = total[pair]
-    for d in range(1, 8):
-        value = value + rs_in[d]
-    acc[...] = value.reshape(PART * 8, N)
-    for j in range(TM):
-        row_buf[j, :PART] = acc[pl.ds(j, PART, stride=8), :]
-        row_buf[j, PART:] = jnp.zeros((16 - PART, N), jnp.float32)
-    rows = []
-    for d in range(TM):
-        for e in range(2):
-            if d == 0 and e == 0:
-                continue
-            other = (tm + d) % TM
-            copy = remote(
-                row_buf.at[other],
-                rows_in.at[core, tm],
-                row_send.at[d, e],
-                row_recv.at[d, e],
-                (other, 2 * pair + (core + e) % 2),
-            )
-            copy.start()
-            rows.append(copy)
-    rows_in[core, tm] = row_buf[tm]
     blocks = []
     for d in (1, 3, 2, 4, 5, 7, 6):
         other = (tm + d) % TM
         copy = remote(dec.at[other], chan_in.at[tm], dec_send.at[d], dec_recv.at[d], (other, ch))
         copy.start()
         blocks.append(copy)
+    give.wait_recv()
+    total[...] = pick[core] + pick_in[...]
+    sums = []
+    for d in ORDER:
+        copy = remote(
+            total.at[pl.ds(2 * ((y + d) % 4), 2)], rs_in.at[d], rs_send.at[d], rs_recv.at[d], device("y", d)
+        )
+        copy.start()
+        sums.append(copy)
+    for copy in sums:
+        copy.wait_recv()
+    acc[...] = (total[pl.ds(2 * y, 2)] + rs_in[1] + rs_in[2] + rs_in[3]).reshape(2 * PART * 8, N)
+    for n in range(16):
+        row_buf[n, :PART] = acc[pl.ds((n // TM) * PART * 8 + n % TM, PART, stride=8), :]
+        row_buf[n, PART:] = jnp.zeros((16 - PART, N), jnp.float32)
+    rows = []
+    for d in range(1, 16):
+        other = (plane + d) % 16
+        copy = remote(row_buf.at[other], rows_in.at[zl, tm], row_send.at[d], row_recv.at[d], in_plane(other))
+        copy.start()
+        rows.append(copy)
+    rows_in[zl, tm] = row_buf[plane]
     for copy in loads:
         copy.wait()
     for copy in rows:
         copy.wait_recv()
+    halves[core] = rows_in[0] + rows_in[1]
+    swap = remote(halves.at[core], halves.at[core], pick_sem.at[2], pick_sem.at[3], sibling)
+    swap.start()
+    swap.wait_recv()
     place = lax.broadcasted_iota(jnp.int32, (HB, N), 0)
     pieces = []
     for j in range(TM):
-        early = rows_in[0, j, :HB]
+        early = halves[0, j, :HB]
         if j > 0:
-            early = early + jnp.where(place == 0, rows_in[1, j - 1, HB : HB + 1], 0.0)
-        pieces += [early, rows_in[1, j, :HB]]
+            early = early + jnp.where(place == 0, halves[1, j - 1, HB : HB + 1], 0.0)
+        pieces += [early, halves[1, j, :HB]]
     src_all[0, 0, 0] = whiten_series([jnp.concatenate(pieces, axis=0)], first, second, third, last, turn)[0]
 
     REST = pl.ds(1, 3)
@@ -469,44 +466,51 @@
             )
             u = res[:64] + jnp.where(left, res[64:], 0.0)
             v = u + pltpu.roll(u, HALF, 1)
-            prod[pl.ds(pl.multiple_of(n * 32, 32), 32), :] = jnp.where(left[:32], v[:32], v[32:])
+            prod[n] = jnp.where(left[:32], v[:32], v[32:]).reshape(LAG_ROWS, 8, N)
+        part = pl.ds(i * UNROLL, UNROLL)
+        pltpu.make_async_copy(prod.at[part], out_hbm.at[part], out_sem.at[i]).start()
         return carry
 
-    for kind in kinds:
-        for d in ORDER:
+    for d in ORDER:
+        for kind in kinds:
             arrived(kind, (REST, REST, 0), 2, (d,))
             share(kind, (REST, REST, 4 - d))
     settle()
     lax.fori_loop(1, 4, late, 0)
     lax.fori_loop(0, N // UNROLL, slots, 0)
 
-    k_hi = back[0]
-    k_both = jnp.concatenate([back[0], back[1]], axis=1)
-    for r in range(LAG_ROWS):
-        for c in range(8):
-            t = prod[pl.ds(r * 8 + c, N, stride=32), :].T
-            hi, lo = split(jnp.concatenate([t[:NSRC], t[NSRC:]], axis=1))
-            wide = mm(hi, k_both)
-            out_ref[c, :, N * r : N * (r + 1)] = wide[:, :N] + wide[:, N:] + mm(lo, k_hi)
-
+    for i in range(N // UNROLL):
+        part = pl.ds(i * UNROLL, UNROLL)
+        pltpu.make_async_copy(prod.at[part], out_hbm.at[part], out_sem.at[i]).wait()
+    swap.wait_send()
     give.wait_send()
     for copy in sums + rows + blocks + started:
         copy.wait_send()
 
 
+def lags_kernel(prod_ref, back, out_ref):
+    k_hi = back[0]
+    k_both = jnp.concatenate([back[0], back[1]], axis=1)
+    for c in range(8):
+        t = prod_ref[:, 0, c, :].T
+        hi, lo = split(jnp.concatenate([t[:NSRC], t[NSRC:]], axis=1))
+        wide = mm(hi, k_both)
+        out_ref[c] = wide[:, :N] + wide[:, N:] + mm(lo, k_hi)
+
+
 def on_device(strain, fir_taps, source_index):
     tables = series_tables()
     win, back = window_tables()
-    tables = [stack_np(t) for t in tables[:4]] + [tables[4], stack_np(win), stack_np(back)]
+    tables = [stack_np(t) for t in tables[:4]] + [tables[4], stack_np(win)]
     dma = pltpu.SemaphoreType.DMA
     f32 = jnp.float32
     smem = pl.BlockSpec(memory_space=pltpu.SMEM)
     anywhere = pl.BlockSpec(memory_space=pl.ANY)
-    return pl.pallas_call(
+    products = pl.pallas_call(
         kernel,
-        out_shape=jax.ShapeDtypeStruct((8, NSRC, LAG_ROWS * N), f32),
+        out_shape=jax.ShapeDtypeStruct((N, LAG_ROWS, 8, N), f32),
         in_specs=[anywhere, smem, smem] + [anywhere] * len(tables),
-        out_specs=pl.BlockSpec(memory_space=VMEM),
+        out_specs=anywhere,
         scratch_shapes=[
             VMEM((GROUP, N + 4 * N * BLOCKS), f32),
             VMEM((BAND, N), f32),
@@ -514,36 +518,50 @@
             VMEM((2, 8, PART, 8, N), f32),
             VMEM((8, PART, 8, N), f32),
             VMEM((8, PART, 8, N), f32),
-            VMEM((8, PART, 8, N), f32),
-            VMEM((PART * 8, N), f32),
-            VMEM((TM, 16, N), f32),
+            VMEM((4, 2, PART, 8, N), f32),
+            VMEM((2 * PART * 8, N), f32),
+            VMEM((16, 16, N), f32),
+            VMEM((2, TM, 16, N), f32),
             VMEM((2, TM, 16, N), f32),
             VMEM((TM, BLOCKS + 1, 8, N), f32),
             VMEM((4, 4, 4, N, N), f32),
             VMEM((2 * N // 8, 64, N), f32),
             VMEM((N, N, 2 * N), jnp.bfloat16),
             VMEM((2 * N // 8, 8 * NSRC, N), f32),
-            VMEM((N * 32, N), f32),
+            VMEM((N, LAG_ROWS, 8, N), f32),
         ]
         + [VMEM(t.shape, jnp.dtype(t.dtype)) for t in tables]
         + [
             dma((1 + len(tables),)),
-            dma((1,)),
             dma((2,)),
+            dma((4,)),
             dma((TM,)),
             dma((TM,)),
-            dma((8,)),
-            dma((8,)),
-            dma((TM, 2)),
-            dma((TM, 2)),
+            dma((4,)),
+            dma((4,)),
+            dma((16,)),
+            dma((16,)),
         ]
         + [dma((81,))] * 2
-        + [dma((27,))] * 2,
+        + [dma((27,))] * 2
+        + [dma((N // UNROLL,))],
         compiler_params=pltpu.CompilerParams(
             collective_id=0, has_side_effects=True, vmem_limit_bytes=VMEM_LIMIT
         ),
         name="interferometry",
     )(strain, fir_taps, source_index, *tables)
+    return pl.pallas_call(
+        lags_kernel,
+        grid=(LAG_ROWS,),
+        out_shape=jax.ShapeDtypeStruct((8, NSRC, LAG_ROWS * N), f32),
+        in_specs=[
+            pl.BlockSpec((N, 1, 8, N), lambda r: (0, r, 0, 0)),
+            pl.BlockSpec((2, 2 * N, N), lambda r: (0, 0, 0)),
+        ],
+        out_specs=pl.BlockSpec((8, NSRC, N), lambda r: (0, 0, r)),
+        compiler_params=pltpu.CompilerParams(vmem_limit_bytes=VMEM_LIMIT),
+        name="lags",
+    )(products, stack_np(back))
 
 
 def solution(mesh):

time: 58.2 us -> 56.4 us (0.969)
  local copies, waits for them, and re-layouts: 2.26 us -> 0 us
  Pallas kernels: 55.3 us -> 56.2 us
    unnamed x1 -> x0, local copies, waits for them, and re-layouts: 2.26 us -> none
    pallas_call x1 -> x2, Pallas kernels: 55.3 us -> 56.2 us  [the longest x1 51.6 us: on_device(): pl.pallas_call(kernel, out_shape=jax.ShapeDtypeStruct((N, LAG_ROWS, 8, N)...]
where the time goes in v4:
time: 56.4 us; the launch traced here: 56.2 us
  Pallas kernels  56.2 us (100%)
    pallas_call x1, Pallas kernels, on_device(): pl.pallas_call(kernel, out_shape=jax.ShapeDtypeStruct((N, LAG_ROWS, 8, N)...  51.6 us
    pallas_call x1, Pallas kernels, on_device(): pl.pallas_call(lags_kernel, grid=(LAG_ROWS,), out_shape=jax.ShapeDtypeStr...  4.61 us

profile of v4, /device:TPU:1, one launch (start us, length us, event | category | flops | bytes accessed | tf_op | source)
XLA Modules:
  0.0 56.2 jit_solution(9360652990773166310)
XLA Ops:
  0.0 51.6 %interferometry.1.prod_ref = f32[128,4,8,128]{3,2,1,0:T(8,128)} custom-call(f32[64,8192]{1,0:T(8,128)} %strain_hbm.1, f32[64]{0:T(128)} %taps_ref.1, s32[64]{0:T(128)} %index_ref.1, bf16[2,128,128]{2,1,0:T(8,128)(2,1)} %constant.14.clone.first_hbm, bf16[2,256,256]{2,1,0:T(8,128)(2,1)} %constant.15.clone.second_hbm, ...), custom_call_target="tpu_custom_call" | custom-call | tf_op jit(solution)/shard_map/interferometry/pallas_call | solution.py:509
  51.6 4.6 %lags.1 = f32[8,64,512]{2,1,0:T(8,128)} custom-call(f32[128,4,8,128]{3,2,1,0:T(8,128)} %interferometry.1.prod_ref, bf16[2,256,128]{2,1,0:T(8,128)(2,1)} %constant.20.clone.back), custom_call_target="tpu_custom_call" | custom-call | tf_op jit(solution)/shard_map/lags/pallas_call | solution.py:553

commit v5 on v4

--- a/solution.py
+++ b/solution.py
@@ -24,7 +24,7 @@
 BAND = 5 * N
 HB = BLOCKS // 2
 PART = HB + 1
-KINDS = ((0, 24, "xyz"), (24, 24, "yzx"), (48, 16, "zxy"))
+KINDS = ((0, 24, "xyz"), (24, 16, "yzx"), (40, 24, "zxy"))
 ORDER = (1, 3, 2)
 UNROLL = 64
 VMEM_LIMIT = 56 * 1024 * 1024
@@ -391,14 +391,14 @@
     for kind in kinds:
         arrived(kind, (0, 0, 0), 0)
         send_on(kind, (REST, 0, 0), 1)
-        share(kind, (REST, 0, 0))
     for kind in kinds:
         arrived(kind, (0, 0, 0), 1)
         send_on(kind, (REST, 0, 0), 2)
         send_on(kind, (0, REST, 0), 2)
-        share(kind, (0, REST, 0))
     for kind in kinds:
         arrived(kind, (0, 0, 0), 2)
+        share(kind, (REST, 0, 0))
+        share(kind, (0, REST, 0))
         share(kind, (0, 0, REST))
     own_blocks.wait()
     for copy in blocks:
@@ -407,6 +407,7 @@
     for kind in kinds:
         arrived(kind, (REST, 0, 0), 1)
         send_on(kind, (REST, REST, 0), 2)
+    for kind in kinds:
         share(kind, (REST, REST, 0))
     channels(4)
     lax.fori_loop(0, N // 8, channel_slots, 0)
@@ -440,10 +441,6 @@
         ry = jnp.where(t < 4, t, 0)
         rz = jnp.where(t < 4, 0, t - 3)
         transform([(ry, rz, rx) for rx in range(1, 4)])
-        return carry
-
-    def late(ry, carry):
-        transform([(ry, rz, rx) for rz in range(1, 4) for rx in range(1, 4)])
         return carry
 
     lax.fori_loop(0, 4, column, 0)
@@ -466,9 +463,9 @@
             )
             u = res[:64] + jnp.where(left, res[64:], 0.0)
             v = u + pltpu.roll(u, HALF, 1)
-            prod[n] = jnp.where(left[:32], v[:32], v[32:]).reshape(LAG_ROWS, 8, N)
+            prod[:, n] = jnp.where(left[:32], v[:32], v[32:]).reshape(LAG_ROWS, 8, N)
         part = pl.ds(i * UNROLL, UNROLL)
-        pltpu.make_async_copy(prod.at[part], out_hbm.at[part], out_sem.at[i]).start()
+        pltpu.make_async_copy(prod.at[:, part], out_hbm.at[:, part], out_sem.at[i]).start()
         return carry
 
     for d in ORDER:
@@ -476,26 +473,42 @@
             arrived(kind, (REST, REST, 0), 2, (d,))
             share(kind, (REST, REST, 4 - d))
     settle()
-    lax.fori_loop(1, 4, late, 0)
+    for ry in (1, 2, 3):
+        transform([(ry, rz, rx) for rz in (1, 2, 3) for rx in (1, 2, 3)])
     lax.fori_loop(0, N // UNROLL, slots, 0)
 
     for i in range(N // UNROLL):
         part = pl.ds(i * UNROLL, UNROLL)
-        pltpu.make_async_copy(prod.at[part], out_hbm.at[part], out_sem.at[i]).wait()
+        pltpu.make_async_copy(prod.at[:, part], out_hbm.at[:, part], out_sem.at[i]).wait()
     swap.wait_send()
     give.wait_send()
     for copy in sums + rows + blocks + started:
         copy.wait_send()
 
 
-def lags_kernel(prod_ref, back, out_ref):
+def lags_kernel(prod_hbm, back_hbm, out_hbm, prod, back, out, in_sem, out_sem):
+    table = pltpu.make_async_copy(back_hbm, back, in_sem.at[LAG_ROWS])
+    table.start()
+    loads = [pltpu.make_async_copy(prod_hbm.at[r], prod.at[r], in_sem.at[r]) for r in range(LAG_ROWS)]
+    for copy in loads:
+        copy.start()
+    table.wait()
     k_hi = back[0]
     k_both = jnp.concatenate([back[0], back[1]], axis=1)
-    for c in range(8):
-        t = prod_ref[:, 0, c, :].T
-        hi, lo = split(jnp.concatenate([t[:NSRC], t[NSRC:]], axis=1))
-        wide = mm(hi, k_both)
-        out_ref[c] = wide[:, :N] + wide[:, N:] + mm(lo, k_hi)
+    for r in range(LAG_ROWS):
+        loads[r].wait()
+        for c0 in range(0, 8, 4):
+            turned = [prod[r, :, c0 + c, :].T for c in range(4)]
+            hi, lo = split(jnp.concatenate([jnp.concatenate([t[:NSRC], t[NSRC:]], axis=1) for t in turned], axis=0))
+            wide = mm(hi, k_both)
+            value = wide[:, :N] + wide[:, N:] + mm(lo, k_hi)
+            out[c0 : c0 + 4, :, N * r : N * (r + 1)] = value.reshape(4, NSRC, N)
+            if r == LAG_ROWS - 1:
+                part = pl.ds(c0, 4)
+                pltpu.make_async_copy(out.at[part], out_hbm.at[part], out_sem.at[c0 // 4]).start()
+    for c0 in range(0, 8, 4):
+        part = pl.ds(c0, 4)
+        pltpu.make_async_copy(out.at[part], out_hbm.at[part], out_sem.at[c0 // 4]).wait()
 
 
 def on_device(strain, fir_taps, source_index):
@@ -508,7 +521,7 @@
     anywhere = pl.BlockSpec(memory_space=pl.ANY)
     products = pl.pallas_call(
         kernel,
-        out_shape=jax.ShapeDtypeStruct((N, LAG_ROWS, 8, N), f32),
+        out_shape=jax.ShapeDtypeStruct((LAG_ROWS, N, 8, N), f32),
         in_specs=[anywhere, smem, smem] + [anywhere] * len(tables),
         out_specs=anywhere,
         scratch_shapes=[
@@ -528,7 +541,7 @@
             VMEM((2 * N // 8, 64, N), f32),
             VMEM((N, N, 2 * N), jnp.bfloat16),
             VMEM((2 * N // 8, 8 * NSRC, N), f32),
-            VMEM((N, LAG_ROWS, 8, N), f32),
+            VMEM((LAG_ROWS, N, 8, N), f32),
         ]
         + [VMEM(t.shape, jnp.dtype(t.dtype)) for t in tables]
         + [
@@ -552,13 +565,16 @@
     )(strain, fir_taps, source_index, *tables)
     return pl.pallas_call(
         lags_kernel,
-        grid=(LAG_ROWS,),
         out_shape=jax.ShapeDtypeStruct((8, NSRC, LAG_ROWS * N), f32),
-        in_specs=[
-            pl.BlockSpec((N, 1, 8, N), lambda r: (0, r, 0, 0)),
-            pl.BlockSpec((2, 2 * N, N), lambda r: (0, 0, 0)),
+        in_specs=[anywhere, anywhere],
+        out_specs=anywhere,
+        scratch_shapes=[
+            VMEM((LAG_ROWS, N, 8, N), f32),
+            VMEM((2, 2 * N, N), jnp.bfloat16),
+            VMEM((8, NSRC, LAG_ROWS * N), f32),
+            dma((LAG_ROWS + 1,)),
+            dma((2,)),
         ],
-        out_specs=pl.BlockSpec((8, NSRC, N), lambda r: (0, 0, r)),
         compiler_params=pltpu.CompilerParams(vmem_limit_bytes=VMEM_LIMIT),
         name="lags",
     )(products, stack_np(back))

time: 56.4 us -> 55.1 us (0.977)
  Pallas kernels: 56.2 us -> 54.9 us
    pallas_call x2, Pallas kernels: 56.2 us -> 54.9 us  [the longest x1 50.9 us: on_device(): pl.pallas_call(kernel, out_shape=jax.ShapeDtypeStruct((LAG_ROWS, N, 8, N)...]
where the time goes in v5:
time: 55.1 us; the launch traced here: 54.9 us
  Pallas kernels  54.9 us (100%)
    pallas_call x1, Pallas kernels, on_device(): pl.pallas_call(kernel, out_shape=jax.ShapeDtypeStruct((LAG_ROWS, N, 8, N)...  50.9 us
    pallas_call x1, Pallas kernels, on_device(): pl.pallas_call(lags_kernel, out_shape=jax.ShapeDtypeStruct((8, NSRC, LAG_...  3.99 us

profile of v5, /device:TPU:1, one launch (start us, length us, event | category | flops | bytes accessed | tf_op | source)
XLA Modules:
  0.0 54.9 jit_solution(2946163010312540027)
XLA Ops:
  0.0 50.9 %interferometry.1.prod_hbm = f32[4,128,8,128]{3,2,1,0:T(8,128)} custom-call(f32[64,8192]{1,0:T(8,128)} %strain_hbm.1, f32[64]{0:T(128)} %taps_ref.1, s32[64]{0:T(128)} %index_ref.1, bf16[2,128,128]{2,1,0:T(8,128)(2,1)} %constant.14.clone.first_hbm, bf16[2,256,256]{2,1,0:T(8,128)(2,1)} %constant.15.clone.second_hbm, ...), custom_call_target="tpu_custom_call" | custom-call | tf_op jit(solution)/shard_map/interferometry/pallas_call | solution.py:522
  50.9 4.0 %lags.1 = f32[8,64,512]{2,1,0:T(8,128)} custom-call(f32[4,128,8,128]{3,2,1,0:T(8,128)} %interferometry.1.prod_hbm, bf16[2,256,128]{2,1,0:T(8,128)(2,1)} %constant.20.clone.back_hbm), custom_call_target="tpu_custom_call" | custom-call | tf_op jit(solution)/shard_map/lags/pallas_call | solution.py:566

commit v6 on v5

--- a/solution.py
+++ b/solution.py
@@ -186,13 +186,20 @@
     for copy in loads:
         copy.start()
 
+    ring_x = [x] + [(x + d) % 4 for d in (1, 2, 3)]
+    ring_y = [y] + [(y + d) % 4 for d in (1, 2, 3)]
+    ring_z = [z] + [(z + d) % 4 for d in (1, 2, 3)]
+    part_y = [16 * v for v in ring_y]
+    part_z = [8 * (v % 2) + 4 * (v // 2) for v in ring_z]
+    devices = {("x", d): (zh * 4 + ring_x[d], ch) for d in (1, 2, 3)}
+    devices.update({("y", d): (tm, ring_y[d] * 4 + zl * 2 + core) for d in (1, 2, 3)})
+    devices.update(
+        {("z", d): ((ring_z[d] // 2) * 4 + x, y * 4 + (ring_z[d] % 2) * 2 + core) for d in (1, 2, 3)}
+    )
+    own_rows = core * HALF
+
     def device(axis, d):
-        if axis == "x":
-            return (zh * 4 + (x + d) % 4, ch)
-        if axis == "y":
-            return (tm, ((y + d) % 4) * 4 + zl * 2 + core)
-        other = (z + d) % 4
-        return ((other // 2) * 4 + x, y * 4 + (other % 2) * 2 + core)
+        return devices[axis, d]
 
     sibling = (tm, 2 * pair + 1 - core)
     plane = 8 * zl + tm
@@ -262,7 +269,7 @@
     sums = []
     for d in ORDER:
         copy = remote(
-            total.at[pl.ds(2 * ((y + d) % 4), 2)], rs_in.at[d], rs_send.at[d], rs_recv.at[d], device("y", d)
+            total.at[pl.ds(2 * ring_y[d], 2)], rs_in.at[d], rs_send.at[d], rs_recv.at[d], device("y", d)
         )
         copy.start()
         sums.append(copy)
@@ -301,7 +308,7 @@
     def region(kind, offsets):
         start, size, order = KINDS[kind]
         at = dict(zip(order, offsets))
-        return src_all.at[at["y"], at["z"], at["x"], pl.ds(core * HALF + start, size)]
+        return src_all.at[at["y"], at["z"], at["x"], pl.ds(own_rows + start, size)]
 
     counts = [{}, {}]
 
@@ -425,26 +432,31 @@
         hi, lo = split(jnp.concatenate([src_all[ry, rz, rx] for ry, rz, rx in places], axis=1))
         rows = []
         for ry, rz, rx in places:
-            z_s = (z + rz) % 4
-            source = 8 * (2 * ((y + ry) % 4) + z_s % 2) + 4 * (z_s // 2) + (x + rx) % 4
+            source = part_y[ry] + part_z[rz] + ring_x[rx]
             rows.append(pl.ds(pl.multiple_of(source * 8, 8), 8))
         res = mm(w_both, jnp.concatenate([hi, lo], axis=0)) + mm(w_lo, hi)
         for i in range(2 * N // 8):
             for e, at in enumerate(rows):
                 spec[i, at, :] = res[8 * i : 8 * i + 8, N * e : N * (e + 1)]
 
-    def column(ry, carry):
-        transform([(ry, rz, 0) for rz in range(4)])
-        return carry
-
-    def early(t, carry):
-        ry = jnp.where(t < 4, t, 0)
-        rz = jnp.where(t < 4, 0, t - 3)
-        transform([(ry, rz, rx) for rx in range(1, 4)])
-        return carry
-
-    lax.fori_loop(0, 4, column, 0)
-    lax.fori_loop(0, 7, early, 0)
+    def hand_over(d):
+        for kind in kinds:
+            arrived(kind, (REST, REST, 0), 2, (d,))
+            share(kind, (REST, REST, 4 - d))
+
+    near = [(ry, rz, 0) for ry in range(4) for rz in range(4)]
+    near += [(ry, rz, rx) for ry, rz in ((0, 0), (1, 0), (2, 0), (3, 0), (0, 1), (0, 2), (0, 3)) for rx in (1, 2, 3)]
+    transform(near[:8])
+    transform(near[8:16])
+    hand_over(1)
+    hand_over(3)
+    transform(near[16:23])
+    transform(near[23:30])
+    transform(near[30:])
+    hand_over(2)
+    settle()
+    for ry in (1, 2, 3):
+        transform([(ry, rz, rx) for rz in (1, 2, 3) for rx in (1, 2, 3)])
 
     left = lax.broadcasted_iota(jnp.int32, (NSRC, N), 1) < HALF
 
@@ -468,13 +480,6 @@
         pltpu.make_async_copy(prod.at[:, part], out_hbm.at[:, part], out_sem.at[i]).start()
         return carry
 
-    for d in ORDER:
-        for kind in kinds:
-            arrived(kind, (REST, REST, 0), 2, (d,))
-            share(kind, (REST, REST, 4 - d))
-    settle()
-    for ry in (1, 2, 3):
-        transform([(ry, rz, rx) for rz in (1, 2, 3) for rx in (1, 2, 3)])
     lax.fori_loop(0, N // UNROLL, slots, 0)
 
     for i in range(N // UNROLL):

time: 55.1 us -> 53.9 us (0.978)
  Pallas kernels: 54.9 us -> 53.7 us
    pallas_call x1, Pallas kernels: 50.9 us -> 49.8 us  [on_device(): pl.pallas_call(kernel, out_shape=jax.ShapeDtypeStruct((LAG_ROWS, N, 8, N)...]
where the time goes in v6:
time: 53.9 us; the launch traced here: 53.8 us
  Pallas kernels  53.7 us (100%)
    pallas_call x1, Pallas kernels, on_device(): pl.pallas_call(kernel, out_shape=jax.ShapeDtypeStruct((LAG_ROWS, N, 8, N)...  49.8 us
    pallas_call x1, Pallas kernels, on_device(): pl.pallas_call(lags_kernel, out_shape=jax.ShapeDtypeStruct((8, NSRC, LAG_...  3.99 us

profile of v6, /device:TPU:1, one launch (start us, length us, event | category | flops | bytes accessed | tf_op | source)
XLA Modules:
  0.0 53.8 jit_solution(3021980950305025440)
XLA Ops:
  0.0 49.8 %interferometry.1.prod_hbm = f32[4,128,8,128]{3,2,1,0:T(8,128)} custom-call(f32[64,8192]{1,0:T(8,128)} %strain_hbm.1, f32[64]{0:T(128)} %taps_ref.1, s32[64]{0:T(128)} %index_ref.1, bf16[2,128,128]{2,1,0:T(8,128)(2,1)} %constant.14.clone.first_hbm, bf16[2,256,256]{2,1,0:T(8,128)(2,1)} %constant.15.clone.second_hbm, ...), custom_call_target="tpu_custom_call" | custom-call | tf_op jit(solution)/shard_map/interferometry/pallas_call | solution.py:527
  49.8 4.0 %lags.1 = f32[8,64,512]{2,1,0:T(8,128)} custom-call(f32[4,128,8,128]{3,2,1,0:T(8,128)} %interferometry.1.prod_hbm, bf16[2,256,128]{2,1,0:T(8,128)(2,1)} %constant.20.clone.back_hbm), custom_call_target="tpu_custom_call" | custom-call | tf_op jit(solution)/shard_map/lags/pallas_call | solution.py:571

commit v7 on v6

--- a/solution.py
+++ b/solution.py
@@ -476,14 +476,16 @@
             u = res[:64] + jnp.where(left, res[64:], 0.0)
             v = u + pltpu.roll(u, HALF, 1)
             prod[:, n] = jnp.where(left[:32], v[:32], v[32:]).reshape(LAG_ROWS, 8, N)
-        part = pl.ds(i * UNROLL, UNROLL)
-        pltpu.make_async_copy(prod.at[:, part], out_hbm.at[:, part], out_sem.at[i]).start()
+            if k % 32 == 31:
+                part = pl.ds(i * UNROLL + k - 31, 32)
+                sem = out_sem.at[i * (UNROLL // 32) + k // 32]
+                pltpu.make_async_copy(prod.at[:, part], out_hbm.at[:, part], sem).start()
         return carry
 
     lax.fori_loop(0, N // UNROLL, slots, 0)
 
-    for i in range(N // UNROLL):
-        part = pl.ds(i * UNROLL, UNROLL)
+    for i in range(N // 32):
+        part = pl.ds(i * 32, 32)
         pltpu.make_async_copy(prod.at[:, part], out_hbm.at[:, part], out_sem.at[i]).wait()
     swap.wait_send()
     give.wait_send()
@@ -562,7 +564,7 @@
         ]
         + [dma((81,))] * 2
         + [dma((27,))] * 2
-        + [dma((N // UNROLL,))],
+        + [dma((N // 32,))],
         compiler_params=pltpu.CompilerParams(
             collective_id=0, has_side_effects=True, vmem_limit_bytes=VMEM_LIMIT
         ),

time: 53.9 us -> 53.7 us (level)
  no operation moved by 1% of the time
where the time goes in v7:
time: 53.7 us; the launch traced here: 53.6 us
  Pallas kernels  53.6 us (100%)
    pallas_call x1, Pallas kernels, on_device(): pl.pallas_call(kernel, out_shape=jax.ShapeDtypeStruct((LAG_ROWS, N, 8, N)...  49.6 us
    pallas_call x1, Pallas kernels, on_device(): pl.pallas_call(lags_kernel, out_shape=jax.ShapeDtypeStruct((8, NSRC, LAG_...  3.99 us

profile of v7, /device:TPU:1, one launch (start us, length us, event | category | flops | bytes accessed | tf_op | source)
XLA Modules:
  0.0 53.6 jit_solution(4455299561158299504)
XLA Ops:
  0.0 49.6 %interferometry.1.prod_hbm = f32[4,128,8,128]{3,2,1,0:T(8,128)} custom-call(f32[64,8192]{1,0:T(8,128)} %strain_hbm.1, f32[64]{0:T(128)} %taps_ref.1, s32[64]{0:T(128)} %index_ref.1, bf16[2,128,128]{2,1,0:T(8,128)(2,1)} %constant.14.clone.first_hbm, bf16[2,256,256]{2,1,0:T(8,128)(2,1)} %constant.15.clone.second_hbm, ...), custom_call_target="tpu_custom_call" | custom-call | tf_op jit(solution)/shard_map/interferometry/pallas_call | solution.py:529
  49.6 4.0 %lags.1 = f32[8,64,512]{2,1,0:T(8,128)} custom-call(f32[4,128,8,128]{3,2,1,0:T(8,128)} %interferometry.1.prod_hbm, bf16[2,256,128]{2,1,0:T(8,128)(2,1)} %constant.20.clone.back_hbm), custom_call_target="tpu_custom_call" | custom-call | tf_op jit(solution)/shard_map/lags/pallas_call | solution.py:573
